TPU v7x, 128 devices: a whole 4x4x4 slice. The times are simulated.
128 devices in a mesh: lat: 4 (over x), lon: 32 (over y, z, core).
Axes of the slice: x: 4, y: 4, z: 4, core: 2. Of those that a mesh axis runs over, the one named last changes fastest.
Arguments:
- velocity_old: float32 [2, 1024, 8192], P(None, 'lat', 'lon'), may hold values from -3 to 3
- wind_stress: float32 [2, 1024, 8192], P(None, 'lat', 'lon'), may hold values from -3 to 3
- strength: float32 [1024, 8192], P('lat', 'lon'), may hold values from 0.3 to 3
- ice_mass: float32 [1024, 8192], P('lat', 'lon'), may hold values from 0.5 to 2
- ice_mask: int32 [8, 64], P('lat', 'lon'), may hold values from 0 to 1, as said below
- block_owner: int32 [8, 64], P('lat', 'lon'), may hold values from 0 to 3, as said below
- block_slot: int32 [8, 64], P('lat', 'lon'), may hold values from 0 to 1
Outputs:
- velocity: float32 [2, 1024, 8192], P(None, 'lat', 'lon')
- held_velocity: float32 [8, 32, 2, 128, 128], P('lat', 'lon')
Inputs may be any that keep to these rules, and one draw needn't show every extreme that they name: `ice_mask`: in every group of 2 block columns of one longitude tile, exactly 8 blocks are ice, among them all blocks of the first 2 block rows. Over the ice blocks of one such group, block_owner * 2 + block_slot takes each value 0 to 7 exactly once; on open-water blocks both are arbitrary within their ranges.
All inputs are finite; a program needn't handle non-finite values.
Results may differ from a plain program's by a relative error of at most 0.0008.
Values sent between devices are 32-bit elements; how exact they have to be, the bound alone decides.
A program may use at most 128 MiB of HBM per device.

v0:
```python
import jax
import jax.numpy as jnp
from jax import lax
from jax.sharding import PartitionSpec as P

BS = 128
BR = 2
BC = 2
KRYLOV = 5
NEWTON = 2
CAP = 2


dmin_sq = 0.04
ellipse_sq = 4.0
drag_coef = 0.5
coriolis = 0.3
tiny_sq = 1e-06


def padded(x, sides, width):
    for axis, dim in sides:
        size, length = (lax.axis_size(axis), x.shape[dim])
        up = [(i, (i + 1) % size) for i in range(size)]
        down = [(j, i) for i, j in up]
        last = lax.slice_in_dim(x, length - width, length, axis=dim)
        leading = lax.slice_in_dim(x, 0, width, axis=dim)
        before = lax.ppermute(last, axis, up)
        after = lax.ppermute(leading, axis, down)
        x = jnp.concatenate([before, x, after], axis=dim)
    return x


def slope_x(field):
    return (field[..., 1:-1, 2:] - field[..., 1:-1, :-2]) * 0.5


def slope_y(field):
    return (field[..., 2:, 1:-1] - field[..., :-2, 1:-1]) * 0.5


def strain_rates(flow_wide):
    flow_east = flow_wide[..., 0, :, :]
    flow_north = flow_wide[..., 1, :, :]
    return (
        slope_x(flow_east),
        slope_y(flow_north),
        0.5 * (slope_y(flow_east) + slope_x(flow_north)),
    )


def viscosities(widened):
    normal_xx, normal_yy, shear_rate = strain_rates(widened[..., 0:2, :, :])
    pressure_mid = widened[..., 2, 1:-1, 1:-1]
    strain_sum = normal_xx + normal_yy
    differ = normal_xx - normal_yy
    squared = (
        strain_sum * strain_sum + (differ * differ + 4.0 * shear_rate * shear_rate) / ellipse_sq
    )
    delta_rate = jnp.sqrt(squared + dmin_sq)
    bulk_visc = pressure_mid / (2.0 * delta_rate)
    visc_slope = bulk_visc / (2.0 * delta_rate * delta_rate)
    return (bulk_visc, visc_slope, strain_sum, differ, shear_rate, pressure_mid)


def divergence(stress_xx, stress_yy, stress_xy):
    return (slope_x(stress_xx) + slope_y(stress_xy), slope_x(stress_xy) + slope_y(stress_yy))


def stress_force(bulk_visc, strain_sum, differ, shear_rate, pressure_mid):
    shear_visc = bulk_visc / ellipse_sq
    return divergence(
        bulk_visc * strain_sum + shear_visc * differ - 0.5 * pressure_mid,
        bulk_visc * strain_sum - shear_visc * differ - 0.5 * pressure_mid,
        2.0 * shear_visc * shear_rate,
    )


def tangent_force(wide_dir, bulk_visc, visc_slope, strain_sum, differ, shear_rate):
    change_xx, change_yy, change_shear = strain_rates(wide_dir)
    change_total = change_xx + change_yy
    change_differ = change_xx - change_yy
    change_squared = (
        2.0 * strain_sum * change_total
        + (2.0 * differ * change_differ + 8.0 * shear_rate * change_shear) / ellipse_sq
    )
    change_bulk = -visc_slope * change_squared
    return divergence(
        change_bulk * (strain_sum + differ / ellipse_sq)
        + bulk_visc * (change_total + change_differ / ellipse_sq),
        change_bulk * (strain_sum - differ / ellipse_sq)
        + bulk_visc * (change_total - change_differ / ellipse_sq),
        2.0 * (change_bulk * shear_rate + bulk_visc * change_shear) / ellipse_sq,
    )


def inertia(flow_now, ice_mass, force_east, force_north):
    flow_east = flow_now[..., 0, :, :]
    flow_north = flow_now[..., 1, :, :]
    along_first = (
        ice_mass * flow_east - coriolis * ice_mass * flow_north + drag_coef * flow_east - force_east
    )
    along_second = (
        ice_mass * flow_north
        + coriolis * ice_mass * flow_east
        + drag_coef * flow_north
        - force_north
    )
    return jnp.stack([along_first, along_second], axis=-3)


def least_squares(hessen, initial_norm):
    upper = hessen
    target_vec = jnp.zeros((KRYLOV + 1,), jnp.float32).at[0].set(initial_norm)
    for column in range(KRYLOV):
        top_entry = upper[column, column]
        below_entry = upper[column + 1, column]
        radius = jnp.sqrt(top_entry * top_entry + below_entry * below_entry)
        cosine = top_entry / radius
        sine_part = below_entry / radius
        first_row = upper[column]
        second_row = upper[column + 1]
        upper = upper.at[column].set(cosine * first_row + sine_part * second_row)
        upper = upper.at[column + 1].set(cosine * second_row - sine_part * first_row)
        first_entry = target_vec[column]
        second_entry = target_vec[column + 1]
        target_vec = target_vec.at[column].set(cosine * first_entry + sine_part * second_entry)
        target_vec = target_vec.at[column + 1].set(cosine * second_entry - sine_part * first_entry)
    weights = jnp.zeros((KRYLOV,), jnp.float32)
    for column in reversed(range(KRYLOV)):
        known = jnp.sum(upper[column, column + 1 :] * weights[column + 1 :])
        weights = weights.at[column].set((target_vec[column] - known) / upper[column, column])
    return weights


def inner_product(first_vec, second_vec):
    return jnp.sum(first_vec * second_vec)


def global_squares(vector):
    return lax.psum(inner_product(vector, vector), ("lat", "lon"))


def krylov_solve(linear_map, target_vec):
    initial_norm = jnp.sqrt(global_squares(target_vec) + tiny_sq)
    krylov_basis = [target_vec / initial_norm]
    hessen = jnp.zeros((KRYLOV + 1, KRYLOV), jnp.float32)
    for column in range(KRYLOV):
        mapped = linear_map(krylov_basis[column])
        local_dots = jnp.stack([inner_product(vector, mapped) for vector in krylov_basis])
        coeffs = lax.psum(local_dots, ("lat", "lon"))
        for previous in range(column + 1):
            mapped = mapped - coeffs[previous] * krylov_basis[previous]
        length = jnp.sqrt(global_squares(mapped) + tiny_sq)
        hessen = hessen.at[: column + 1, column].set(coeffs).at[column + 1, column].set(length)
        krylov_basis.append(mapped / length)
    weights = least_squares(hessen, initial_norm)
    update = weights[0] * krylov_basis[0]
    for column in range(1, KRYLOV):
        update = update + weights[column] * krylov_basis[column]
    return update


def solve_newton(flow_now, flow_old, wind_stress, pressure, ice_mass, ice_weight, widen):
    for newton_step in range(NEWTON):
        widened = widen(jnp.concatenate([flow_now, pressure[..., None, :, :]], axis=-3))
        bulk_visc, visc_slope, strain_sum, differ, shear_rate, pressure_mid = viscosities(widened)
        force_east, force_north = stress_force(
            bulk_visc, strain_sum, differ, shear_rate, pressure_mid
        )
        residual = ice_weight * (
            inertia(flow_now, ice_mass, force_east, force_north)
            - ice_mass[..., None, :, :] * flow_old
            - wind_stress
        )

        def linear_map(direction):
            change_east, change_north = tangent_force(
                widen(direction), bulk_visc, visc_slope, strain_sum, differ, shear_rate
            )
            return ice_weight * inertia(direction, ice_mass, change_east, change_north)

        flow_now = flow_now + krylov_solve(linear_map, -residual)
    return flow_now


def clear_poles(widened, dim, width):
    row_count = widened.shape[dim]
    row_index = jnp.arange(row_count)
    at_pole = lax.axis_index("lat") == 0
    at_equator = lax.axis_index("lat") == lax.axis_size("lat") - 1
    keep_rows = jnp.logical_not(
        at_pole & (row_index < width) | at_equator & (row_index >= row_count - width)
    )
    shape_list = [1] * widened.ndim
    shape_list[dim] = row_count
    return widened * keep_rows.astype(widened.dtype).reshape(shape_list)


def tile_blocks(tile_field):
    channels = tile_field.shape[0]
    shaped = tile_field.reshape(channels, BR, BS, BC, BS)
    return shaped.transpose(1, 3, 0, 2, 4).reshape(BR * BC, channels, BS, BS)


def pick_rows(values, source_of, present):
    picked = jnp.take(values, source_of, axis=0)
    return picked * present.reshape((-1,) + (1,) * (values.ndim - 1))


def on_device(velocity_old, wind_stress, strength, ice_mass, ice_mask, block_owner, block_slot):
    lat_count = lax.axis_size("lat")
    slot_count = lat_count * CAP
    ice_flat = ice_mask.reshape(-1).astype(jnp.float32)
    target_slot = (block_owner * CAP + block_slot).reshape(-1)
    matches = (target_slot[None, :] == jnp.arange(slot_count)[:, None]) & (ice_flat[None, :] > 0.5)
    present = jnp.sum(matches.astype(jnp.float32), axis=1)
    source_of = jnp.sum(matches.astype(jnp.int32) * jnp.arange(BR * BC)[None, :], axis=1)
    ice_cells = jnp.repeat(jnp.repeat(ice_mask.astype(jnp.float32), BS, axis=0), BS, axis=1)

    def widen(field):
        widened = padded(field, (("lat", 1), ("lon", 2)), 2)
        return clear_poles(widened, 1, 2)

    velocity = solve_newton(
        velocity_old * ice_cells,
        velocity_old,
        wind_stress,
        strength * ice_cells,
        ice_mass,
        ice_cells,
        widen,
    )
    picked = pick_rows(tile_blocks(velocity), source_of, present)
    picked = picked.reshape((lat_count, CAP) + picked.shape[1:])
    arrived = lax.all_to_all(picked, "lat", split_axis=0, concat_axis=0, tiled=True)
    anchors = lax.all_to_all(
        present.reshape(lat_count, CAP), "lat", split_axis=0, concat_axis=0, tiled=True
    )
    held_flow, anchors = (jnp.sum(arrived, axis=0), anchors)
    return (velocity, held_flow[:, None])


def solution(mesh):
    return jax.shard_map(
        on_device,
        mesh=mesh,
        in_specs=(
            P(None, "lat", "lon"),
            P(None, "lat", "lon"),
            P("lat", "lon"),
            P("lat", "lon"),
            P("lat", "lon"),
            P("lat", "lon"),
            P("lat", "lon"),
        ),
        out_specs=(P(None, "lat", "lon"), P("lat", "lon", None, None, None)),
        check_vma=False,
    )
```

profile of v0, /device:TPU:1, one launch (start us, length us, event | category | flops | bytes accessed | tf_op | source)
XLA Modules:
  0.0 1882.3 jit_solution(8421645694696478829)
XLA Ops:
  1.9 3.4 collective-permute-start.1
  6.1 2.9 collective-permute-done
  13.0 5.5 collective-permute-done.3
  23.3 69.4 %psum.154 = f32[]{:T(128)} all-reduce(f32[]{:T(128)} %get-tuple-element.971), channel_id=1, replica_groups=mesh['lat'=4,'lon'=32] {'lat','lon'}, use_global_device_ids=true, to_apply=%region_1.0 | all-reduce | flops 1 | bytes 8 | tf_op jit(solution)/shard_map/psum | solution.py:141
  102.0 3.4 collective-permute-done.7
  105.9 2.8 multiply_add_fusion.19
  110.9 66.0 %psum.155 = f32[1]{0:T(128)} all-reduce(f32[1]{0:T(128)} %bitcast.16), channel_id=1, replica_groups=mesh['lat'=4,'lon'=32] {'lat','lon'}, use_global_device_ids=true, to_apply=%region_3.0 | all-reduce | flops 1 | bytes 8 | tf_op jit(solution)/shard_map/psum | solution.py:151
  179.0 62.7 %psum.156 = f32[]{:T(128)} all-reduce(f32[]{:T(128)} %multiply_reduce_fusion.39), channel_id=1, replica_groups=mesh['lat'=4,'lon'=32] {'lat','lon'}, use_global_device_ids=true, to_apply=%region_5.0 | all-reduce | flops 1 | bytes 8 | tf_op jit(solution)/shard_map/psum | solution.py:141
  246.1 2.9 collective-permute-done.8
  249.1 2.3 collective-permute-start.11
  251.5 3.6 collective-permute-done.11
  263.6 67.0 %psum.157 = f32[2]{0:T(128)S(1)} all-reduce(f32[2]{0:T(128)S(1)} %pad_maximum_fusion.16), channel_id=1, replica_groups=mesh['lat'=4,'lon'=32] {'lat','lon'}, use_global_device_ids=true, to_apply=%region_9.0 | all-reduce | flops 2 | bytes 16 | tf_op jit(solution)/shard_map/psum | solution.py:151
  331.1 3.8 multiply_reduce_fusion.36
  334.9 62.5 %psum.158 = f32[]{:T(128)} all-reduce(f32[]{:T(128)} %get-tuple-element.956), channel_id=1, replica_groups=mesh['lat'=4,'lon'=32] {'lat','lon'}, use_global_device_ids=true, to_apply=%region_11.0 | all-reduce | flops 1 | bytes 8 | tf_op jit(solution)/shard_map/psum | solution.py:141
  401.1 2.9 collective-permute-done.12
  404.2 2.3 collective-permute-start.15
  407.3 2.8 collective-permute-done.15
  418.8 67.2 %psum.159 = f32[3]{0:T(128)S(1)} all-reduce(f32[3]{0:T(128)S(1)} %pad_maximum_fusion.17), channel_id=1, replica_groups=mesh['lat'=4,'lon'=32] {'lat','lon'}, use_global_device_ids=true, to_apply=%region_16.0 | all-reduce | flops 3 | bytes 24 | tf_op jit(solution)/shard_map/psum | solution.py:151
  486.7 5.3 multiply_reduce_fusion.32
  492.0 62.5 %psum.160 = f32[]{:T(128)} all-reduce(f32[]{:T(128)} %get-tuple-element.949), channel_id=1, replica_groups=mesh['lat'=4,'lon'=32] {'lat','lon'}, use_global_device_ids=true, to_apply=%region_18.0 | all-reduce | flops 1 | bytes 8 | tf_op jit(solution)/shard_map/psum | solution.py:141
  564.8 2.2 collective-permute-start.19
  579.6 2.5 pad_maximum_fusion.18
  582.3 67.1 %psum.161 = f32[4]{0:T(128)S(1)} all-reduce(f32[4]{0:T(128)S(1)} %pad_maximum_fusion.18), channel_id=1, replica_groups=mesh['lat'=4,'lon'=32] {'lat','lon'}, use_global_device_ids=true, to_apply=%region_24.0 | all-reduce | flops 4 | bytes 32 | tf_op jit(solution)/shard_map/psum | solution.py:151
  650.0 6.1 multiply_reduce_fusion.27
  656.1 62.9 %psum.162 = f32[]{:T(128)} all-reduce(f32[]{:T(128)} %get-tuple-element.942), channel_id=1, replica_groups=mesh['lat'=4,'lon'=32] {'lat','lon'}, use_global_device_ids=true, to_apply=%region_26.0 | all-reduce | flops 1 | bytes 8 | tf_op jit(solution)/shard_map/psum | solution.py:141
  729.4 2.2 collective-permute-start.23
  742.6 2.4 multiply_reduce_fusion.22
  745.0 3.2 stack.258
  748.3 67.1 %psum.163 = f32[5]{0:T(128)S(1)} all-reduce(f32[5]{0:T(128)S(1)} %stack.258), channel_id=1, replica_groups=mesh['lat'=4,'lon'=32] {'lat','lon'}, use_global_device_ids=true, to_apply=%region_33.0 | all-reduce | flops 5 | bytes 40 | tf_op jit(solution)/shard_map/psum | solution.py:151
  818.0 5.8 multiply_reduce_fusion.21
  825.3 64.2 %psum.164 = f32[]{:T(128)} all-reduce(f32[]{:T(128)} %multiply_reduce_fusion.21), channel_id=1, replica_groups=mesh['lat'=4,'lon'=32] {'lat','lon'}, use_global_device_ids=true, to_apply=%region_35.0 | all-reduce | flops 1 | bytes 8 | tf_op jit(solution)/shard_map/psum | solution.py:141
  931.2 4.0 add_add_fusion.1
  943.3 5.8 collective-permute-done.27
  953.1 65.6 %psum.165 = f32[]{:T(128)} all-reduce(f32[]{:T(128)} %get-tuple-element.929), channel_id=1, replica_groups=mesh['lat'=4,'lon'=32] {'lat','lon'}, use_global_device_ids=true, to_apply=%region_40.0 | all-reduce | flops 1 | bytes 8 | tf_op jit(solution)/shard_map/psum | solution.py:141
  1027.2 4.1 collective-permute-done.31
  1031.8 2.8 multiply_add_fusion.9
  1036.8 66.0 %psum.166 = f32[1]{0:T(128)} all-reduce(f32[1]{0:T(128)} %bitcast.134), channel_id=1, replica_groups=mesh['lat'=4,'lon'=32] {'lat','lon'}, use_global_device_ids=true, to_apply=%region_42.0 | all-reduce | flops 1 | bytes 8 | tf_op jit(solution)/shard_map/psum | solution.py:151
  1104.2 62.6 %psum.167 = f32[]{:T(128)} all-reduce(f32[]{:T(128)} %multiply_reduce_fusion.18), channel_id=1, replica_groups=mesh['lat'=4,'lon'=32] {'lat','lon'}, use_global_device_ids=true, to_apply=%region_44.0 | all-reduce | flops 1 | bytes 8 | tf_op jit(solution)/shard_map/psum | solution.py:141
  1171.9 3.1 collective-permute-done.32
  1176.2 2.3 collective-permute-start.35
  1178.6 3.5 collective-permute-done.35
  1190.1 67.0 %psum.168 = f32[2]{0:T(128)S(1)} all-reduce(f32[2]{0:T(128)S(1)} %pad_maximum_fusion.19), channel_id=1, replica_groups=mesh['lat'=4,'lon'=32] {'lat','lon'}, use_global_device_ids=true, to_apply=%region_47.0 | all-reduce | flops 2 | bytes 16 | tf_op jit(solution)/shard_map/psum | solution.py:151
  1257.7 3.7 multiply_reduce_fusion.15
  1261.4 62.5 %psum.169 = f32[]{:T(128)} all-reduce(f32[]{:T(128)} %get-tuple-element.914), channel_id=1, replica_groups=mesh['lat'=4,'lon'=32] {'lat','lon'}, use_global_device_ids=true, to_apply=%region_49.0 | all-reduce | flops 1 | bytes 8 | tf_op jit(solution)/shard_map/psum | solution.py:141
  1327.6 2.9 collective-permute-done.36
  1330.7 2.3 collective-permute-start.39
  1333.0 3.6 collective-permute-done.39
  1345.3 67.0 %psum.170 = f32[3]{0:T(128)S(1)} all-reduce(f32[3]{0:T(128)S(1)} %pad_maximum_fusion.20), channel_id=1, replica_groups=mesh['lat'=4,'lon'=32] {'lat','lon'}, use_global_device_ids=true, to_apply=%region_53.0 | all-reduce | flops 3 | bytes 24 | tf_op jit(solution)/shard_map/psum | solution.py:151
  1412.9 5.1 multiply_reduce_fusion.11
  1418.0 62.9 %psum.171 = f32[]{:T(128)} all-reduce(f32[]{:T(128)} %get-tuple-element.907), channel_id=1, replica_groups=mesh['lat'=4,'lon'=32] {'lat','lon'}, use_global_device_ids=true, to_apply=%region_55.0 | all-reduce | flops 1 | bytes 8 | tf_op jit(solution)/shard_map/psum | solution.py:141
  1486.6 2.8 collective-permute-done.40
  1491.3 2.2 collective-permute-start.43
  1506.1 2.6 pad_maximum_fusion.21
  1508.9 66.9 %psum.172 = f32[4]{0:T(128)S(1)} all-reduce(f32[4]{0:T(128)S(1)} %pad_maximum_fusion.21), channel_id=1, replica_groups=mesh['lat'=4,'lon'=32] {'lat','lon'}, use_global_device_ids=true, to_apply=%region_60.0 | all-reduce | flops 4 | bytes 32 | tf_op jit(solution)/shard_map/psum | solution.py:151
  1576.5 6.2 multiply_reduce_fusion.6
  1582.7 62.5 %psum.173 = f32[]{:T(128)} all-reduce(f32[]{:T(128)} %get-tuple-element.900), channel_id=1, replica_groups=mesh['lat'=4,'lon'=32] {'lat','lon'}, use_global_device_ids=true, to_apply=%region_62.0 | all-reduce | flops 1 | bytes 8 | tf_op jit(solution)/shard_map/psum | solution.py:141
  1655.6 2.2 collective-permute-start.47
  1668.8 2.5 multiply_reduce_fusion.1
  1671.3 3.2 stack.295
  1674.6 67.2 %psum.174 = f32[5]{0:T(128)S(1)} all-reduce(f32[5]{0:T(128)S(1)} %stack.295), channel_id=1, replica_groups=mesh['lat'=4,'lon'=32] {'lat','lon'}, use_global_device_ids=true, to_apply=%region_68.0 | all-reduce | flops 5 | bytes 40 | tf_op jit(solution)/shard_map/psum | solution.py:151
  1744.5 6.0 multiply_reduce_fusion
  1752.0 64.2 %psum.175 = f32[]{:T(128)} all-reduce(f32[]{:T(128)} %multiply_reduce_fusion), channel_id=1, replica_groups=mesh['lat'=4,'lon'=32] {'lat','lon'}, use_global_device_ids=true, to_apply=%region_70.0 | all-reduce | flops 1 | bytes 8 | tf_op jit(solution)/shard_map/psum | solution.py:141
  1858.1 4.7 add_add_fusion
  1865.0 16.4 all_to_all.5
  (478 shorter events, 219.2 us)
Async XLA Ops:
  1.8 16.7 copy-start.35
  1.9 4.2 collective-permute-start.1
  5.3 3.7 collective-permute-start
  9.2 9.3 collective-permute-start.3
  11.4 7.1 collective-permute-start.2
  20.2 235.4 %copy-start.1 = (f32[258,258]{1,0:T(8,128)}, f32[258,258]{1,0:T(8,128)S(1)}, u32[]{:S(2)}) copy-start(f32[258,258]{1,0:T(8,128)S(1)} %get-tuple-element.976) | copy-start | bytes 798772
  22.5 72.6 %copy-start.70 = (s32[2]{0:T(128)S(1)}, s32[2]{0:T(128)}, u32[]{:S(2)}) copy-start(s32[2]{0:T(128)} %constant.1561.clone.1) | copy-start | bytes 28
  93.5 7.8 copy-start.69
  93.5 2.5 collective-permute-start.5
  94.0 3.7 collective-permute-start.4
  97.9 7.5 collective-permute-start.7
  99.8 5.6 collective-permute-start.6
  110.1 68.1 %copy-start.68 = (s32[2]{0:T(128)S(1)}, s32[2]{0:T(128)}, u32[]{:S(2)}) copy-start(s32[2]{0:T(128)} %constant.1563.clone.1) | copy-start | bytes 28
  243.1 2.9 collective-permute-start.9
  245.3 3.7 collective-permute-start.8
  249.1 6.0 collective-permute-start.11
  251.5 3.6 collective-permute-start.10
  398.2 2.9 collective-permute-start.13
  400.3 3.7 collective-permute-start.12
  404.2 6.0 collective-permute-start.15
  406.5 3.6 collective-permute-start.14
  414.5 2.3 copy-start.61
  557.1 4.2 collective-permute-start.17
  559.2 3.7 collective-permute-start.16
  564.8 6.2 collective-permute-start.19
  567.1 4.0 collective-permute-start.18
  721.6 5.5 collective-permute-start.21
  723.7 3.7 collective-permute-start.20
  729.4 6.2 collective-permute-start.23
  731.6 4.0 collective-permute-start.22
  931.2 8.4 copy-start.36
  935.1 15.9 copy-start.15
  935.2 2.5 collective-permute-start.25
  935.8 3.8 collective-permute-start.24
  939.9 9.3 collective-permute-start.27
  941.9 7.2 collective-permute-start.26
  950.8 231.9 %copy-start.5 = (f32[258,258]{1,0:T(8,128)}, f32[258,258]{1,0:T(8,128)S(1)}, u32[]{:S(2)}) copy-start(f32[258,258]{1,0:T(8,128)S(1)} %get-tuple-element.934) | copy-start | bytes 798772
  1019.4 2.5 collective-permute-start.29
  1019.9 3.7 collective-permute-start.28
  1023.8 7.5 collective-permute-start.31
  1025.7 5.5 collective-permute-start.30
  1036.0 68.1 %copy-start.65 = (s32[2,2]{1,0:T(2,128)S(1)}, s32[2,2]{1,0:T(2,128)}, u32[]{:S(2)}) copy-start(s32[2,2]{1,0:T(2,128)} %param.157) | copy-start | bytes 52
  1036.0 68.1 %copy-start.66 = (s32[2,2]{1,0:T(2,128)S(1)}, s32[2,2]{1,0:T(2,128)}, u32[]{:S(2)}) copy-start(s32[2,2]{1,0:T(2,128)} %param.156) | copy-start | bytes 52
  1104.2 67.2 %copy-start.67 = (s32[2,2]{1,0:T(2,128)S(1)}, s32[2,2]{1,0:T(2,128)}, u32[]{:S(2)}) copy-start(s32[2,2]{1,0:T(2,128)} %param.155) | copy-start | bytes 52
  1169.0 2.9 collective-permute-start.33
  1171.2 3.9 collective-permute-start.32
  1171.5 10.6 copy-start.46
  1176.2 6.0 collective-permute-start.35
  1178.5 3.6 collective-permute-start.34
  1186.4 2.2 copy-start.57
  1324.7 2.9 collective-permute-start.37
  1326.8 3.7 collective-permute-start.36
  1330.7 6.0 collective-permute-start.39
  1333.0 3.6 collective-permute-start.38
  1341.0 2.3 copy-start.59
  1483.6 3.0 collective-permute-start.41
  1485.7 3.7 collective-permute-start.40
  1491.3 6.2 collective-permute-start.43
  1493.6 4.0 collective-permute-start.42
  1647.8 5.5 collective-permute-start.45
  1649.9 3.7 collective-permute-start.44
  1655.6 6.2 collective-permute-start.47
  1657.8 4.0 collective-permute-start.46
  1744.5 113.7 %copy-start.16 = (f32[2,256,256]{2,1,0:T(8,128)S(1)}, f32[2,256,256]{2,1,0:T(8,128)}, u32[]{:S(2)}) copy-start(f32[2,256,256]{2,1,0:T(8,128)} %copy-done.15) | copy-start | bytes 1572868
  (55 other events, 70.0 us)
where the time goes:
time: 1900 us; the launch traced here: 1880 us
  blocking collectives  1450 us (76%)
  other arithmetic  164 us (9%)
  local copies, waits for them, and re-layouts  77 us (4%)
  between operations  69.7 us (4%)
  waiting for transfers between devices  64.1 us (3%)
  starting transfers between devices  58.1 us (3%)
    psum x12, blocking collectives, global_squares(): return lax.psum(inner_product(vector, vector), ('lat', 'lon'))  764 us
    psum x10, blocking collectives, krylov_solve(): coeffs = lax.psum(local_dots, ('lat', 'lon'))  668 us
    reduce_sum x22, other arithmetic, inner_product(): return jnp.sum(first_vec * second_vec)  62.4 us
    ppermute x24, starting transfers between devices, padded(): after = lax.ppermute(leading, axis, down)  48.4 us
    ppermute x24, waiting for transfers between devices, padded(): after = lax.ppermute(leading, axis, down)  39.1 us
  transfers between devices with their start and end apart: 48, of which 32 were waited for; matrix products, arithmetic and copies ran while one was open for 1% of the time, Pallas kernels for 0%

commit v1 on v0

v1 whole, which is shorter than its diff:
```python
import functools

import jax
import jax.numpy as jnp
from jax import lax
from jax.experimental import pallas as pl
from jax.experimental.pallas import tpu as pltpu
from jax.sharding import PartitionSpec as P

MESH = pl.DeviceIdType.MESH
F32 = jnp.float32

KRYLOV = 5
TINY_SQ = 1e-6
LAT = 4
LON = 32

ROWS = 320
TOP = 32
BOT = 288
HALO = 24
OWN_STRIPS = 32

WIDTHS = (22, 22, 22, 20, 20, 20)
OFFSETS = (0, 22, 44, 66, 86, 106)

N_DOTS = 21
N_SUMS = 24


def lanes(shape):
    return lax.broadcasted_iota(jnp.int32, shape, len(shape) - 1)


def rows8(start):
    return pl.ds(start, 8)


def diff_x(f):
    lane = lanes((1, 8, 128))
    right = pltpu.roll(f, 127, 2)
    left = pltpu.roll(f, 1, 2)
    right_next = jnp.concatenate([right[1:], right[:1]], axis=0)
    left_next = jnp.concatenate([left[2:], left[:2]], axis=0)
    return jnp.where(lane == 127, right_next, right) - jnp.where(lane == 0, left_next, left)


def diff_x_rough(f):
    return pltpu.roll(f, 127, 2) - pltpu.roll(f, 1, 2)


def coefficients(sum_rate, differ, shear, pressure):
    q = 0.25 * (sum_rate * sum_rate) + 0.0625 * (differ * differ + shear * shear)
    inv = lax.rsqrt(q + 0.04)
    bulk = 0.5 * pressure * inv
    weight = inv * jnp.sqrt(0.5 * bulk)
    eighth = 0.125 * weight
    return 0.5 * bulk, 0.125 * bulk, (0.5 * weight) * sum_rate, eighth * differ, eighth * shear


def spectrum_sums(m2, gs, gf, ge, mass, turn):
    diag = mass + 1.5 * m2 - (gs * gs + gf * gf + ge * ge)
    c11 = 2.5 * m2 - 2.0 * (gs + gf) * (gs + gf)
    c22 = 2.5 * m2 - 2.0 * (gs - gf) * (gs - gf)
    c33 = 2.0 * m2 - 8.0 * ge * ge
    spread = diag * diag + turn * turn + 0.0625 * (c11 * c11 + c22 * c22) + 0.03125 * (c33 * c33)
    return diag, spread


def splat(row, index):
    return jnp.broadcast_to(row[:, index : index + 1], (1, 128))


def wide(row):
    return jnp.broadcast_to(row, (8, 128))


def small_solve(gram, mid, rho):
    def dot(u, gv):
        total = None
        for x, y in zip(u, gv):
            if x is not None:
                total = x * y if total is None else total + x * y
        return total

    def times_gram(u, count):
        return [dot(u, [gram[i][j] for j in range(6)]) for i in range(count)]

    def apply(c):
        out = [None] * 6
        for k, x in enumerate(c):
            if x is None:
                continue
            if k < 5:
                terms = [(k + 1, x), (k, mid * x)]
                if k > 0:
                    terms.append((k - 1, rho[k] * x))
                for at, term in terms:
                    out[at] = term if out[at] is None else out[at] + term
        return out

    beta = jnp.sqrt(gram[0][0] + TINY_SQ)
    basis = [[1.0 / beta] + [None] * 5]
    upper = []
    cosines, sines = [], []
    target = [beta]
    for j in range(KRYLOV):
        u = apply(basis[j])
        gu = times_gram(u, j + 2)
        coeffs = [dot(basis[i][: j + 2], gu) for i in range(j + 1)]
        for i in range(j + 1):
            u = [
                x if y is None else x - coeffs[i] * y
                for x, y in zip(u, basis[i])
            ]
        gu = times_gram(u, j + 2)
        square = jnp.maximum(dot(u[: j + 2], gu), 0.0)
        length = jnp.sqrt(square + TINY_SQ)
        inv_length = 1.0 / length
        basis.append([None if x is None else x * inv_length for x in u])
        column = coeffs + [length]
        for i in range(j):
            a, b = column[i], column[i + 1]
            column[i] = cosines[i] * a + sines[i] * b
            column[i + 1] = cosines[i] * b - sines[i] * a
        a, b = column[j], column[j + 1]
        inv_radius = 1.0 / jnp.sqrt(a * a + b * b)
        cosine, sine = a * inv_radius, b * inv_radius
        cosines.append(cosine)
        sines.append(sine)
        column[j] = cosine * a + sine * b
        upper.append(column[: j + 1])
        target.append(-sine * target[j])
        target[j] = cosine * target[j]
    weights = [None] * KRYLOV
    for j in reversed(range(KRYLOV)):
        known = target[j]
        for k in range(j + 1, KRYLOV):
            known = known - upper[k][j] * weights[k]
        weights[j] = known / upper[j][j]
    out = []
    for k in range(KRYLOV):
        total = None
        for j in range(k, KRYLOV):
            term = weights[j] * basis[j][k]
            total = term if total is None else total + term
        out.append(total)
    return out


def kernel(
    ice_ref, owner_ref, slot_ref, vel_ref, wind_ref, strength_ref, mass_ref,
    out_ref, held_ref,
    st_vel, st_wind, st_strength, st_mass,
    fields, local, coef, stress, krylov,
    pack_e, pack_w, got_l, got_r, sums,
    buf_a, buf_b, send_blocks, recv_blocks, held_buf,
    in_sem, halo_send, halo_recv, ar_send, ar_recv, held_send, held_recv, out_sem,
):
    lat, lon = lax.axis_index("lat"), lax.axis_index("lon")
    north, south = lax.rem(lat + LAT - 1, LAT), lax.rem(lat + 1, LAT)
    east, west = lax.rem(lon + 1, LON), lax.rem(lon + LON - 1, LON)
    core = lax.rem(lon, 2)
    chip = lon // 2
    rank_a = lat * 2 + core
    rank_b = chip

    peers_a = []
    for i in (4, 5, 2, 3, 6, 7, 1):
        other = lax.rem(rank_a + i, 8)
        peers_a.append((other // 2, chip * 2 + lax.rem(other, 2)))
    peers_b = []
    for i in (10, 9, 11, 6, 8, 2, 14, 7, 5, 13, 1, 3, 15, 4, 12):
        peers_b.append((lat, lax.rem(rank_b + i, 16) * 2 + core))
    halo_peers = [(lat, east), (lat, west), (north, east), (north, west), (south, east), (south, west)]

    barrier = pltpu.get_barrier_semaphore()
    greeted = peers_b + peers_a + halo_peers
    for peer in greeted:
        pl.semaphore_signal(barrier, inc=1, device_id=peer, device_id_type=MESH)

    loads = []
    for t in range(2):
        cols = pl.ds(128 * t, 128)
        loads.append(pltpu.make_async_copy(vel_ref.at[:, :, cols], st_vel.at[:, t], in_sem.at[t]))
        loads.append(pltpu.make_async_copy(wind_ref.at[:, :, cols], st_wind.at[:, t], in_sem.at[2 + t]))
        loads.append(pltpu.make_async_copy(strength_ref.at[:, cols], st_strength.at[t], in_sem.at[4 + t]))
        loads.append(pltpu.make_async_copy(mass_ref.at[:, cols], st_mass.at[t], in_sem.at[6 + t]))
    for copy in loads:
        copy.start()
    for copy in loads:
        copy.wait()

    lane8 = lanes((8, 128))
    ice = [[ice_ref[i, j].astype(F32) for j in range(2)] for i in range(2)]
    for half in range(2):

        def prepare(s, carry, half=half):
            src = pl.multiple_of(8 * s, 8)
            dst = pl.multiple_of(TOP + 8 * s, 8)
            for t in range(2):
                w = ice[half][t]
                mass = st_mass[t, rows8(src), :] * w
                v_e = st_vel[0, t, rows8(src), :]
                v_n = st_vel[1, t, rows8(src), :]
                values = (
                    v_e * w,
                    v_n * w,
                    st_strength[t, rows8(src), :] * w,
                    mass,
                    mass * v_e + w * st_wind[0, t, rows8(src), :],
                    mass * v_n + w * st_wind[1, t, rows8(src), :],
                )
                for f in range(6):
                    fields[f, t, rows8(dst), :] = values[f]
                local[0, t, rows8(dst), :] = mass + 0.5 * w
                local[1, t, rows8(dst), :] = 0.3 * mass
                local[2, t, rows8(dst), :] = jnp.zeros((8, 128), F32) + 0.5 * w
                packed = None
                for f in range(6):
                    turn = (OFFSETS[f] if t == 0 else OFFSETS[f] + WIDTHS[f]) % 128
                    rolled = values[f] if turn == 0 else pltpu.roll(values[f], turn, 1)
                    packed = rolled if f == 0 else jnp.where(lane8 >= OFFSETS[f], rolled, packed)
                (pack_w if t == 0 else pack_e)[rows8(src), :] = packed
            return carry

        lax.fori_loop(16 * half, 16 * half + 16, prepare, 0)

    pl.semaphore_wait(barrier, len(greeted))

    own_top, own_bot = pl.ds(TOP, HALO), pl.ds(BOT - HALO, HALO)
    halo_top, halo_bot = pl.ds(TOP - HALO, HALO), pl.ds(BOT, HALO)
    own_rows = pl.ds(TOP, 256)
    src_top, src_bot = pl.ds(0, HALO), pl.ds(256 - HALO, HALO)
    plan = [
        (fields.at[:, pl.ds(0, 2), own_top, :], fields.at[:, pl.ds(0, 2), halo_bot, :], (north, lon)),
        (fields.at[:, pl.ds(0, 2), own_bot, :], fields.at[:, pl.ds(0, 2), halo_top, :], (south, lon)),
        (pack_e.at[src_top, :], got_l.at[halo_bot, :], (north, east)),
        (pack_w.at[src_top, :], got_r.at[halo_bot, :], (north, west)),
        (pack_e.at[src_bot, :], got_l.at[halo_top, :], (south, east)),
        (pack_w.at[src_bot, :], got_r.at[halo_top, :], (south, west)),
        (pack_e, got_l.at[own_rows, :], (lat, east)),
        (pack_w, got_r.at[own_rows, :], (lat, west)),
    ]
    halo_copies = []
    for i, (src, dst, peer) in enumerate(plan):
        copy = pltpu.make_async_remote_copy(
            src_ref=src, dst_ref=dst, send_sem=halo_send.at[i], recv_sem=halo_recv.at[i],
            device_id=peer, device_id_type=MESH,
        )
        copy.start()
        halo_copies.append(copy)

    def reduce_a_start(inst, row):
        buf_a[inst, rank_a] = row
        for peer in peers_a:
            pltpu.make_async_remote_copy(
                src_ref=buf_a.at[inst, rank_a], dst_ref=buf_a.at[inst, rank_a],
                send_sem=ar_send.at[inst, 0], recv_sem=ar_recv.at[inst, 0],
                device_id=peer, device_id_type=MESH,
            ).start()

    def reduce_b_start(inst):
        waited = buf_a.at[inst, pl.ds(0, 7)]
        pltpu.make_async_copy(waited, waited, ar_recv.at[inst, 0]).wait()
        row = buf_a[inst, 0]
        for i in range(1, 8):
            row = row + buf_a[inst, i]
        buf_b[inst, rank_b] = row
        for peer in peers_b:
            pltpu.make_async_remote_copy(
                src_ref=buf_b.at[inst, rank_b], dst_ref=buf_b.at[inst, rank_b],
                send_sem=ar_send.at[inst, 1], recv_sem=ar_recv.at[inst, 1],
                device_id=peer, device_id_type=MESH,
            ).start()

    def reduce_end(inst):
        waited = buf_b.at[inst, pl.ds(0, 15)]
        pltpu.make_async_copy(waited, waited, ar_recv.at[inst, 1]).wait()
        parts = [buf_b[inst, i] for i in range(16)]
        while len(parts) > 1:
            parts = [x + y for x, y in zip(parts[::2], parts[1::2])]
        return parts[0]

    def put_sum(index, acc):
        sums[index : index + 1, :] = jnp.sum(acc, axis=0, keepdims=True)

    def packed_sums(count):
        m = sums[0:count, :]
        total = jnp.sum(m, axis=1, keepdims=True)
        sub = lax.broadcasted_iota(jnp.int32, (count, 128), 0)
        spread = jnp.where(lanes((count, 128)) == sub, total, 0.0)
        return jnp.sum(spread, axis=0, keepdims=True)

    def estimate_pass(alpha):
        both = pl.ds(0, 2)

        def at(c, r):
            flow = fields[c, both, rows8(r), :]
            return flow if alpha is None else flow + alpha * krylov[0, c, both, rows8(r), :]

        def body(i, carry):
            diag_acc, spread_acc, ice_acc = carry
            r = pl.multiple_of(TOP + 8 + 16 * i, 8)
            x_e, x_n = diff_x_rough(at(0, r)), diff_x_rough(at(1, r))
            y_e, y_n = at(0, r + 1) - at(0, r - 1), at(1, r + 1) - at(1, r - 1)
            m2, _, gs, gf, ge = coefficients(x_e + y_n, x_e - y_n, y_e + x_n, fields[2, both, rows8(r), :])
            diag, spread = spectrum_sums(
                m2, gs, gf, ge, local[0, both, rows8(r), :], local[1, both, rows8(r), :]
            )
            weight = local[2, both, rows8(r), :]
            return (
                diag_acc + (diag[0] + diag[1]),
                spread_acc + (spread[0] + spread[1]),
                ice_acc + 2.0 * (weight[0] + weight[1]),
            )

        zero = jnp.zeros((8, 128), F32)
        return lax.fori_loop(0, 15, body, (zero, zero, zero))

    def basis_of(row, at):
        diag, spread, count = splat(row, at), splat(row, at + 1), splat(row, at + 2)
        inv = 1.0 / jnp.maximum(count, 1.0)
        mid = diag * inv
        return mid, jnp.maximum(spread * inv - mid * mid, 0.01)

    for i, acc in enumerate(estimate_pass(None)):
        put_sum(i, acc)
    reduce_a_start(0, packed_sums(8))

    for copy in halo_copies:
        copy.wait_recv()

    keep_top = jnp.where(lat == 0, 0.0, 1.0).astype(F32)
    keep_bot = jnp.where(lat == LAT - 1, 0.0, 1.0).astype(F32)

    def put_local(t, r, mass):
        w = jnp.where(mass > 0.0, 1.0, 0.0)
        local[0, t, rows8(r), :] = mass + 0.5 * w
        local[1, t, rows8(r), :] = 0.3 * mass
        local[2, t, rows8(r), :] = 0.5 * w

    def unpack(lo, hi, keep):
        def body(s, carry):
            r = pl.multiple_of(8 + 8 * s, 8)
            left, right = got_l[rows8(r), :], got_r[rows8(r), :]
            for f in range(6):
                turn_l = (128 - OFFSETS[f] - WIDTHS[f]) % 128
                turn_r = (128 - OFFSETS[f]) % 128
                from_l = left if turn_l == 0 else pltpu.roll(left, turn_l, 1)
                from_r = right if turn_r == 0 else pltpu.roll(right, turn_r, 1)
                merged = jnp.where(lane8 < 64, from_r, from_l)
                if keep is not None:
                    merged = merged * keep
                    for t in range(2):
                        kept = fields[f, t, rows8(r), :] * keep
                        fields[f, t, rows8(r), :] = kept
                        if f == 3:
                            put_local(t, r, kept)
                fields[f, 2, rows8(r), :] = merged
                if f == 3:
                    put_local(2, r, merged)
            return carry

        lax.fori_loop(lo, hi, body, 0)

    unpack(0, 3, keep_top)
    unpack(3, 35, None)
    unpack(35, 38, keep_bot)

    reduce_b_start(0)

    def strips(halo):
        return 3 - halo, 35 + halo

    def viscous_pass(halo):
        def body(s, carry):
            r = pl.multiple_of(8 + 8 * s, 8)
            x_e, x_n = diff_x(fields[0, :, rows8(r), :]), diff_x(fields[1, :, rows8(r), :])
            y_e = fields[0, :, rows8(r + 1), :] - fields[0, :, rows8(r - 1), :]
            y_n = fields[1, :, rows8(r + 1), :] - fields[1, :, rows8(r - 1), :]
            pressure = fields[2, :, rows8(r), :]
            total, differ, shear = x_e + y_n, x_e - y_n, y_e + x_n
            values = coefficients(total, differ, shear, pressure)
            for i in range(5):
                coef[i, :, rows8(r), :] = values[i]
            p, n = values[0] * total - 0.5 * pressure, values[1] * differ
            stress[0, :, rows8(r), :] = p + n
            stress[1, :, rows8(r), :] = p - n
            stress[2, :, rows8(r), :] = values[1] * shear
            return carry

        lo, hi = strips(halo)
        lax.fori_loop(lo, hi, body, 0)

    def tangent_pass(k, halo):
        def body(s, carry):
            r = pl.multiple_of(8 + 8 * s, 8)
            x_e, x_n = diff_x(krylov[k, 0, :, rows8(r), :]), diff_x(krylov[k, 1, :, rows8(r), :])
            y_e = krylov[k, 0, :, rows8(r + 1), :] - krylov[k, 0, :, rows8(r - 1), :]
            y_n = krylov[k, 1, :, rows8(r + 1), :] - krylov[k, 1, :, rows8(r - 1), :]
            total, differ, shear = x_e + y_n, x_e - y_n, y_e + x_n
            gs, gf, ge = coef[2, :, rows8(r), :], coef[3, :, rows8(r), :], coef[4, :, rows8(r), :]
            q = gs * total + gf * differ + ge * shear
            m8 = coef[1, :, rows8(r), :]
            p = coef[0, :, rows8(r), :] * total - q * gs
            n = m8 * differ - q * gf
            stress[0, :, rows8(r), :] = p + n
            stress[1, :, rows8(r), :] = p - n
            stress[2, :, rows8(r), :] = m8 * shear - q * ge
            return carry

        lo, hi = strips(halo)
        lax.fori_loop(lo, hi, body, 0)

    def stress_force(r):
        t11, t12 = stress[0, :, rows8(r), :], stress[2, :, rows8(r), :]
        y12 = stress[2, :, rows8(r + 1), :] - stress[2, :, rows8(r - 1), :]
        y22 = stress[1, :, rows8(r + 1), :] - stress[1, :, rows8(r - 1), :]
        half = local[2, :, rows8(r), :]
        return half * (diff_x(t11) + y12), half * (diff_x(t12) + y22)

    def residual_at(r):
        force_e, force_n = stress_force(r)
        mass, turn = local[0, :, rows8(r), :], local[1, :, rows8(r), :]
        a, b = fields[0, :, rows8(r), :], fields[1, :, rows8(r), :]
        r_e = fields[4, :, rows8(r), :] + force_e - (mass * a - turn * b)
        r_n = fields[5, :, rows8(r), :] + force_n - (mass * b + turn * a)
        return r_e, r_n

    def jacobian_at(k, r, mid, rho):
        force_e, force_n = stress_force(r)
        mass, turn = local[0, :, rows8(r), :] - mid, local[1, :, rows8(r), :]
        c, d = krylov[k, 0, :, rows8(r), :], krylov[k, 1, :, rows8(r), :]
        w_e = (mass * c - turn * d) - force_e
        w_n = (mass * d + turn * c) - force_n
        if k > 0:
            w_e = w_e - rho * krylov[k - 1, 0, :, rows8(r), :]
            w_n = w_n - rho * krylov[k - 1, 1, :, rows8(r), :]
        return w_e, w_n

    def vector_pass(make, k, halo):
        stored = k < KRYLOV

        def put(r):
            v_e, v_n = make(r)
            if stored:
                krylov[k, 0, :, rows8(r), :] = v_e
                krylov[k, 1, :, rows8(r), :] = v_n
            return v_e, v_n

        def outer(s, carry):
            put(pl.multiple_of(8 + 8 * s, 8))
            return carry

        def inner(s, accs):
            r = pl.multiple_of(8 + 8 * s, 8)
            v_e, v_n = put(r)
            v_e, v_n = v_e[:2], v_n[:2]
            out = []
            for i in range(k + 1):
                if i < k:
                    u_e = krylov[i, 0, pl.ds(0, 2), rows8(r), :]
                    u_n = krylov[i, 1, pl.ds(0, 2), rows8(r), :]
                else:
                    u_e, u_n = v_e, v_n
                product = u_e * v_e + u_n * v_n
                out.append(accs[i] + (product[0] + product[1]))
            return tuple(out)

        lo, hi = strips(halo)
        if halo:
            lax.fori_loop(lo, 3, outer, 0)
        accs = lax.fori_loop(3, 35, inner, tuple(jnp.zeros((8, 128), F32) for _ in range(k + 1)))
        if halo:
            lax.fori_loop(35, hi, outer, 0)
        return accs

    def dot_index(i, k):
        return k * (k + 1) // 2 + i

    mid = square = None
    for step in range(2):
        viscous_pass(3 - step)
        accs = vector_pass(residual_at, 0, 3 - step)
        put_sum(0, accs[0])
        if step == 0:
            mid, square = basis_of(reduce_end(0), 0)
        rho = [None, 2.0 * square] + [square] * 3
        mid8, rho8 = wide(mid), [None if x is None else wide(x) for x in rho]
        norm0 = accs[0]
        for k in range(KRYLOV):
            tangent_pass(k, ((3, 3, 2, 2, 1), (2, 1, 1, 1, 1))[step][k])
            accs = vector_pass(
                lambda r, k=k: jacobian_at(k, r, mid8, rho8[k]), k + 1, ((3, 2, 2, 2, 0), (1, 1, 1, 1, 0))[step][k]
            )
            for i, acc in enumerate(accs):
                put_sum(dot_index(i, k + 1), acc)
            if step == 0 and k == 0:
                def whole(acc):
                    return jnp.sum(jnp.sum(acc, axis=0, keepdims=True), axis=1, keepdims=True)

                g00, g01, g11 = whole(norm0), whole(accs[0]), whole(accs[1])
                m1 = mid[:, 0:1]
                alpha = (g01 + m1 * g00) / (g11 + 2.0 * m1 * g01 + m1 * m1 * g00 + 1e-12)
                alpha = jnp.broadcast_to(alpha, (8, 128))
                for i, acc in enumerate(estimate_pass(alpha)):
                    put_sum(N_DOTS + i, acc)

        reduce_a_start(1 + step, packed_sums(N_SUMS))
        reduce_b_start(1 + step)
        row = reduce_end(1 + step)
        gram = [[None] * 6 for _ in range(6)]
        for j in range(6):
            for i in range(j + 1):
                gram[i][j] = gram[j][i] = splat(row, dot_index(i, j))
        weights = [wide(x) for x in small_solve(gram, mid, rho)]

        def update(s, carry, step=step, weights=weights):
            r = pl.multiple_of(8 + 8 * s, 8)
            tiles = pl.ds(0, 3 if step == 0 else 2)
            for c in range(2):
                total = fields[c, tiles, rows8(r), :]
                for k in range(KRYLOV):
                    total = total + weights[k] * krylov[k, c, tiles, rows8(r), :]
                fields[c, tiles, rows8(r), :] = total
            return carry

        if step == 0:
            for copy in halo_copies:
                copy.wait_send()
        lo, hi = strips(2 if step == 0 else 0)
        lax.fori_loop(lo, hi, update, 0)
        if step == 0:
            mid, square = basis_of(row, N_DOTS)

    outs = []
    for t in range(2):
        outs.append(
            pltpu.make_async_copy(
                fields.at[pl.ds(0, 2), t, own_rows, :], out_ref.at[:, :, pl.ds(128 * t, 128)], out_sem.at[t]
            )
        )
        outs[-1].start()

    picks = []
    for s in range(8):
        picks.append([])
        for i in range(2):
            for j in range(2):
                hit = (ice_ref[i, j] > 0) & (owner_ref[i, j] * 2 + slot_ref[i, j] == s)
                picks[-1].append(jnp.where(hit, 1.0, 0.0).astype(F32))

    def choose(s, carry):
        src = pl.multiple_of(8 * s, 8)
        for c in range(2):
            blocks = []
            for i in range(2):
                for j in range(2):
                    blocks.append(fields[c, j, rows8(pl.multiple_of(TOP + 128 * i + 8 * s, 8)), :])
            for slot in range(8):
                total = blocks[0] * picks[slot][0]
                for b in range(1, 4):
                    total = total + blocks[b] * picks[slot][b]
                send_blocks[slot // 2, slot % 2, c, rows8(src), :] = total
        return carry

    lax.fori_loop(0, 16, choose, 0)

    held_copies = []
    for i in (2, 1, 3):
        other = lax.rem(lat + i, LAT)
        copy = pltpu.make_async_remote_copy(
            src_ref=send_blocks.at[other], dst_ref=recv_blocks.at[i - 1],
            send_sem=held_send.at[i - 1], recv_sem=held_recv.at[i - 1],
            device_id=(other, lon), device_id_type=MESH,
        )
        copy.start()
        held_copies.append(copy)
    for copy in held_copies:
        copy.wait_recv()

    def collect(s, carry):
        r = pl.multiple_of(8 * s, 8)
        for slot in range(2):
            for c in range(2):
                total = send_blocks[lat, slot, c, rows8(r), :]
                for i in range(3):
                    total = total + recv_blocks[i, slot, c, rows8(r), :]
                held_buf[slot, c, rows8(r), :] = total
        return carry

    lax.fori_loop(0, 16, collect, 0)
    last = pltpu.make_async_copy(held_buf, held_ref.at[:, 0], out_sem.at[2])
    last.start()

    for copy in held_copies:
        copy.wait_send()
    for inst in range(3):
        sent = buf_a.at[inst, pl.ds(0, 7)]
        pltpu.make_async_copy(sent, sent, ar_send.at[inst, 0]).wait()
        sent = buf_b.at[inst, pl.ds(0, 15)]
        pltpu.make_async_copy(sent, sent, ar_send.at[inst, 1]).wait()
    for copy in outs:
        copy.wait()
    last.wait()


def on_device(velocity_old, wind_stress, strength, ice_mass, ice_mask, block_owner, block_slot):
    smem = pl.BlockSpec(memory_space=pltpu.SMEM)
    hbm = pl.BlockSpec(memory_space=pl.ANY)
    field = (3, ROWS, 128)
    velocity, held = pl.pallas_call(
        kernel,
        out_shape=(
            jax.ShapeDtypeStruct((2, 256, 256), F32),
            jax.ShapeDtypeStruct((2, 1, 2, 128, 128), F32),
        ),
        in_specs=[smem] * 3 + [hbm] * 4,
        out_specs=(hbm, hbm),
        scratch_shapes=[
            pltpu.VMEM((2, 2, 256, 128), F32),
            pltpu.VMEM((2, 2, 256, 128), F32),
            pltpu.VMEM((2, 256, 128), F32),
            pltpu.VMEM((2, 256, 128), F32),
            pltpu.VMEM((6,) + field, F32),
            pltpu.VMEM((3,) + field, F32),
            pltpu.VMEM((5,) + field, F32),
            pltpu.VMEM((3,) + field, F32),
            pltpu.VMEM((KRYLOV, 2) + field, F32),
            pltpu.VMEM((256, 128), F32),
            pltpu.VMEM((256, 128), F32),
            pltpu.VMEM((ROWS, 128), F32),
            pltpu.VMEM((ROWS, 128), F32),
            pltpu.VMEM((N_SUMS, 128), F32),
            pltpu.VMEM((3, 8, 1, 128), F32),
            pltpu.VMEM((3, 16, 1, 128), F32),
            pltpu.VMEM((4, 2, 2, 128, 128), F32),
            pltpu.VMEM((3, 2, 2, 128, 128), F32),
            pltpu.VMEM((2, 2, 128, 128), F32),
            pltpu.SemaphoreType.DMA((8,)),
            pltpu.SemaphoreType.DMA((8,)),
            pltpu.SemaphoreType.DMA((8,)),
            pltpu.SemaphoreType.DMA((3, 2)),
            pltpu.SemaphoreType.DMA((3, 2)),
            pltpu.SemaphoreType.DMA((3,)),
            pltpu.SemaphoreType.DMA((3,)),
            pltpu.SemaphoreType.DMA((3,)),
        ],
        compiler_params=pltpu.CompilerParams(
            collective_id=0, has_side_effects=True, vmem_limit_bytes=56 * 1024 * 1024
        ),
    )(ice_mask, block_owner, block_slot, velocity_old, wind_stress, strength, ice_mass)
    return velocity, held


def solution(mesh):
    return jax.shard_map(
        on_device,
        mesh=mesh,
        in_specs=(
            P(None, "lat", "lon"),
            P(None, "lat", "lon"),
            P("lat", "lon"),
            P("lat", "lon"),
            P("lat", "lon"),
            P("lat", "lon"),
            P("lat", "lon"),
        ),
        out_specs=(P(None, "lat", "lon"), P("lat", "lon", None, None, None)),
        check_vma=False,
    )
```

time: 1900 us -> 136 us (0.07)
  blocking collectives: 1450 us -> 0 us
  other arithmetic: 164 us -> 0 us
  Pallas kernels: 0 us -> 133 us
  local copies, waits for them, and re-layouts: 77 us -> 2.62 us
  between operations: 69.7 us -> 0.65 us
  waiting for transfers between devices: 64.1 us -> 0 us
  starting transfers between devices: 58.1 us -> 0 us
    psum x22 -> x0, blocking collectives: 1430 us -> none  [the longest x12 764 us: global_squares(): return lax.psum(inner_product(vector, vector), ('lat', 'lon'))]
    pallas_call x0 -> x1, Pallas kernels: none -> 133 us  [on_device(): pl.pallas_call(kernel, out_shape=(jax.ShapeDtypeStruct((2, 256, 256), F32...]
    reduce_sum x31 -> x0, other arithmetic: 67.6 us -> none  [the longest x22 62.4 us: inner_product(): return jnp.sum(first_vec * second_vec)]
    ppermute x48 -> x0, waiting for transfers between devices: 64.1 us -> none  [the longest x24 39.1 us: padded(): after = lax.ppermute(leading, axis, down)]
    ppermute x48 -> x0, starting transfers between devices: 58.1 us -> none  [the longest x24 48.4 us: padded(): after = lax.ppermute(leading, axis, down)]
    another operation x33 -> x0, other arithmetic: 36.2 us -> none
    add x25 -> x0, other arithmetic: 33.4 us -> none  [the longest x10 22.1 us: tangent_force(): change_bulk * (strain_sum + differ / ellipse_sq)]
    slice x64 -> x0, local copies, waits for them, and re-layouts: 26.9 us -> none  [the longest x10 5.79 us: least_squares(): upper[column, column]]
  transfers between devices with their start and end apart: 48 -> 0, of which waited for: 32 -> 0; matrix products, arithmetic and copies ran while one was open for 1% -> 0% of each run, Pallas kernels for 0% -> 0%
where the time goes in v1:
time: 136 us
  Pallas kernels  133 us (98%)
  local copies, waits for them, and re-layouts  2.62 us (2%)
    pallas_call x1, Pallas kernels, on_device(): pl.pallas_call(kernel, out_shape=(jax.ShapeDtypeStruct((2, 256, 256), F32...  133 us

profile of v1, /device:TPU:1, one launch (start us, length us, event | category | flops | bytes accessed | tf_op | source)
XLA Modules:
  0.0 135.9 jit_solution(9635365042808186961)
XLA Ops:
  0.6 132.7 %shard_map.86 = (f32[2,256,256]{2,1,0:T(8,128)}, f32[2,1,2,128,128]{4,3,2,1,0:T(8,128)}) custom-call(s32[2,2]{1,0:T(2,128)} %ice_ref.1, s32[2,2]{1,0:T(2,128)} %owner_ref.1, s32[2,2]{1,0:T(2,128)} %slot_ref.1, f32[2,256,256]{2,1,0:T(8,128)} %vel_ref.1, f32[2,256,256]{2,1,0:T(8,128)} %wind_ref.1, f32[256,256]{1,0:T(8,128)} %strength_ref.1, f32[256,256]{1,0:T(8,128)} %mass_ref.1), custom_call_target="tpu_custom_call" | custom-call | tf_op jit(solution)/shard_map/pallas_call | solution.py:613
  133.3 0.0 copy-start
  133.3 1.9 %copy.11 = f32[2,256,256]{2,1,0:T(8,128)} copy(f32[2,256,256]{2,1,0:T(8,128)} %get-tuple-element.4) | data formatting | bytes 1048576
  135.2 0.0 copy-done
  135.2 0.7 copy.12
Async XLA Ops:
  133.3 1.9 %copy-start = (f32[2,1,2,128,128]{4,3,2,1,0:T(8,128)S(1)}, f32[2,1,2,128,128]{4,3,2,1,0:T(8,128)}, u32[]{:S(2)}) copy-start(f32[2,1,2,128,128]{4,3,2,1,0:T(8,128)} %get-tuple-element.5) | copy-start | bytes 786436

commit v2 on v1

--- a/solution.py
+++ b/solution.py
@@ -24,6 +24,11 @@
 WIDTHS = (22, 22, 22, 20, 20, 20)
 OFFSETS = (0, 22, 44, 66, 86, 106)
 
+VISC = 4
+TAN = 8
+VEC = 8
+UPD = 4
+
 N_DOTS = 21
 N_SUMS = 24
 
@@ -32,12 +37,33 @@
     return lax.broadcasted_iota(jnp.int32, shape, len(shape) - 1)
 
 
+def sweep(lo, hi, body, carry, strips):
+    count, rest = divmod(hi - lo, strips)
+
+    def step(i, carry):
+        return body(pl.multiple_of(8 + 8 * lo + 8 * strips * i, 8), 8 * strips, carry)
+
+    if count:
+        carry = lax.fori_loop(0, count, step, carry)
+    if rest:
+        carry = body(8 + 8 * (hi - rest), 8 * rest, carry)
+    return carry
+
+
+def fold(x):
+    x = x.reshape(-1, 8, 128)
+    total = x[0]
+    for i in range(1, x.shape[0]):
+        total = total + x[i]
+    return total
+
+
 def rows8(start):
     return pl.ds(start, 8)
 
 
 def diff_x(f):
-    lane = lanes((1, 8, 128))
+    lane = lanes((1,) + f.shape[1:])
     right = pltpu.roll(f, 127, 2)
     left = pltpu.roll(f, 1, 2)
     right_next = jnp.concatenate([right[1:], right[:1]], axis=0)
@@ -374,106 +400,107 @@
         return 3 - halo, 35 + halo
 
     def viscous_pass(halo):
-        def body(s, carry):
-            r = pl.multiple_of(8 + 8 * s, 8)
-            x_e, x_n = diff_x(fields[0, :, rows8(r), :]), diff_x(fields[1, :, rows8(r), :])
-            y_e = fields[0, :, rows8(r + 1), :] - fields[0, :, rows8(r - 1), :]
-            y_n = fields[1, :, rows8(r + 1), :] - fields[1, :, rows8(r - 1), :]
-            pressure = fields[2, :, rows8(r), :]
+        def body(r, n, carry):
+            here, up, down = pl.ds(r, n), pl.ds(r + 1, n), pl.ds(r - 1, n)
+            x_e, x_n = diff_x(fields[0, :, here, :]), diff_x(fields[1, :, here, :])
+            y_e = fields[0, :, up, :] - fields[0, :, down, :]
+            y_n = fields[1, :, up, :] - fields[1, :, down, :]
+            pressure = fields[2, :, here, :]
             total, differ, shear = x_e + y_n, x_e - y_n, y_e + x_n
             values = coefficients(total, differ, shear, pressure)
             for i in range(5):
-                coef[i, :, rows8(r), :] = values[i]
+                coef[i, :, here, :] = values[i]
             p, n = values[0] * total - 0.5 * pressure, values[1] * differ
-            stress[0, :, rows8(r), :] = p + n
-            stress[1, :, rows8(r), :] = p - n
-            stress[2, :, rows8(r), :] = values[1] * shear
+            stress[0, :, here, :] = p + n
+            stress[1, :, here, :] = p - n
+            stress[2, :, here, :] = values[1] * shear
             return carry
 
         lo, hi = strips(halo)
-        lax.fori_loop(lo, hi, body, 0)
+        sweep(lo, hi, body, 0, VISC)
 
     def tangent_pass(k, halo):
-        def body(s, carry):
-            r = pl.multiple_of(8 + 8 * s, 8)
-            x_e, x_n = diff_x(krylov[k, 0, :, rows8(r), :]), diff_x(krylov[k, 1, :, rows8(r), :])
-            y_e = krylov[k, 0, :, rows8(r + 1), :] - krylov[k, 0, :, rows8(r - 1), :]
-            y_n = krylov[k, 1, :, rows8(r + 1), :] - krylov[k, 1, :, rows8(r - 1), :]
+        def body(r, n, carry):
+            here, up, down = pl.ds(r, n), pl.ds(r + 1, n), pl.ds(r - 1, n)
+            x_e, x_n = diff_x(krylov[k, 0, :, here, :]), diff_x(krylov[k, 1, :, here, :])
+            y_e = krylov[k, 0, :, up, :] - krylov[k, 0, :, down, :]
+            y_n = krylov[k, 1, :, up, :] - krylov[k, 1, :, down, :]
             total, differ, shear = x_e + y_n, x_e - y_n, y_e + x_n
-            gs, gf, ge = coef[2, :, rows8(r), :], coef[3, :, rows8(r), :], coef[4, :, rows8(r), :]
+            gs, gf, ge = coef[2, :, here, :], coef[3, :, here, :], coef[4, :, here, :]
             q = gs * total + gf * differ + ge * shear
-            m8 = coef[1, :, rows8(r), :]
-            p = coef[0, :, rows8(r), :] * total - q * gs
+            m8 = coef[1, :, here, :]
+            p = coef[0, :, here, :] * total - q * gs
             n = m8 * differ - q * gf
-            stress[0, :, rows8(r), :] = p + n
-            stress[1, :, rows8(r), :] = p - n
-            stress[2, :, rows8(r), :] = m8 * shear - q * ge
+            stress[0, :, here, :] = p + n
+            stress[1, :, here, :] = p - n
+            stress[2, :, here, :] = m8 * shear - q * ge
             return carry
 
         lo, hi = strips(halo)
-        lax.fori_loop(lo, hi, body, 0)
-
-    def stress_force(r):
-        t11, t12 = stress[0, :, rows8(r), :], stress[2, :, rows8(r), :]
-        y12 = stress[2, :, rows8(r + 1), :] - stress[2, :, rows8(r - 1), :]
-        y22 = stress[1, :, rows8(r + 1), :] - stress[1, :, rows8(r - 1), :]
-        half = local[2, :, rows8(r), :]
+        sweep(lo, hi, body, 0, TAN)
+
+    def stress_force(r, n):
+        here, up, down = pl.ds(r, n), pl.ds(r + 1, n), pl.ds(r - 1, n)
+        t11, t12 = stress[0, :, here, :], stress[2, :, here, :]
+        y12 = stress[2, :, up, :] - stress[2, :, down, :]
+        y22 = stress[1, :, up, :] - stress[1, :, down, :]
+        half = local[2, :, here, :]
         return half * (diff_x(t11) + y12), half * (diff_x(t12) + y22)
 
-    def residual_at(r):
-        force_e, force_n = stress_force(r)
-        mass, turn = local[0, :, rows8(r), :], local[1, :, rows8(r), :]
-        a, b = fields[0, :, rows8(r), :], fields[1, :, rows8(r), :]
-        r_e = fields[4, :, rows8(r), :] + force_e - (mass * a - turn * b)
-        r_n = fields[5, :, rows8(r), :] + force_n - (mass * b + turn * a)
+    def residual_at(r, n):
+        here = pl.ds(r, n)
+        force_e, force_n = stress_force(r, n)
+        mass, turn = local[0, :, here, :], local[1, :, here, :]
+        a, b = fields[0, :, here, :], fields[1, :, here, :]
+        r_e = fields[4, :, here, :] + force_e - (mass * a - turn * b)
+        r_n = fields[5, :, here, :] + force_n - (mass * b + turn * a)
         return r_e, r_n
 
-    def jacobian_at(k, r, mid, rho):
-        force_e, force_n = stress_force(r)
-        mass, turn = local[0, :, rows8(r), :] - mid, local[1, :, rows8(r), :]
-        c, d = krylov[k, 0, :, rows8(r), :], krylov[k, 1, :, rows8(r), :]
+    def jacobian_at(k, r, n, mid, rho):
+        here = pl.ds(r, n)
+        force_e, force_n = stress_force(r, n)
+        mass, turn = local[0, :, here, :] - mid, local[1, :, here, :]
+        c, d = krylov[k, 0, :, here, :], krylov[k, 1, :, here, :]
         w_e = (mass * c - turn * d) - force_e
         w_n = (mass * d + turn * c) - force_n
         if k > 0:
-            w_e = w_e - rho * krylov[k - 1, 0, :, rows8(r), :]
-            w_n = w_n - rho * krylov[k - 1, 1, :, rows8(r), :]
+            w_e = w_e - rho * krylov[k - 1, 0, :, here, :]
+            w_n = w_n - rho * krylov[k - 1, 1, :, here, :]
         return w_e, w_n
 
     def vector_pass(make, k, halo):
         stored = k < KRYLOV
 
-        def put(r):
-            v_e, v_n = make(r)
+        def put(r, n):
+            v_e, v_n = make(r, n)
             if stored:
-                krylov[k, 0, :, rows8(r), :] = v_e
-                krylov[k, 1, :, rows8(r), :] = v_n
+                krylov[k, 0, :, pl.ds(r, n), :] = v_e
+                krylov[k, 1, :, pl.ds(r, n), :] = v_n
             return v_e, v_n
 
-        def outer(s, carry):
-            put(pl.multiple_of(8 + 8 * s, 8))
+        def outer(r, n, carry):
+            put(r, n)
             return carry
 
-        def inner(s, accs):
-            r = pl.multiple_of(8 + 8 * s, 8)
-            v_e, v_n = put(r)
+        def inner(r, n, accs):
+            v_e, v_n = put(r, n)
             v_e, v_n = v_e[:2], v_n[:2]
             out = []
             for i in range(k + 1):
                 if i < k:
-                    u_e = krylov[i, 0, pl.ds(0, 2), rows8(r), :]
-                    u_n = krylov[i, 1, pl.ds(0, 2), rows8(r), :]
+                    u_e = krylov[i, 0, pl.ds(0, 2), pl.ds(r, n), :]
+                    u_n = krylov[i, 1, pl.ds(0, 2), pl.ds(r, n), :]
                 else:
                     u_e, u_n = v_e, v_n
-                product = u_e * v_e + u_n * v_n
-                out.append(accs[i] + (product[0] + product[1]))
+                out.append(accs[i] + fold(u_e * v_e + u_n * v_n))
             return tuple(out)
 
         lo, hi = strips(halo)
         if halo:
-            lax.fori_loop(lo, 3, outer, 0)
-        accs = lax.fori_loop(3, 35, inner, tuple(jnp.zeros((8, 128), F32) for _ in range(k + 1)))
+            sweep(lo, 3, outer, 0, halo)
+        accs = sweep(3, 35, inner, tuple(jnp.zeros((8, 128), F32) for _ in range(k + 1)), VEC)
         if halo:
-            lax.fori_loop(35, hi, outer, 0)
+            sweep(35, hi, outer, 0, halo)
         return accs
 
     def dot_index(i, k):
@@ -487,12 +514,12 @@
         if step == 0:
             mid, square = basis_of(reduce_end(0), 0)
         rho = [None, 2.0 * square] + [square] * 3
-        mid8, rho8 = wide(mid), [None if x is None else wide(x) for x in rho]
+        mid8, rho8 = mid, rho
         norm0 = accs[0]
         for k in range(KRYLOV):
             tangent_pass(k, ((3, 3, 2, 2, 1), (2, 1, 1, 1, 1))[step][k])
             accs = vector_pass(
-                lambda r, k=k: jacobian_at(k, r, mid8, rho8[k]), k + 1, ((3, 2, 2, 2, 0), (1, 1, 1, 1, 0))[step][k]
+                lambda r, n, k=k: jacobian_at(k, r, n, mid8, rho8[k]), k + 1, ((3, 2, 2, 2, 0), (1, 1, 1, 1, 0))[step][k]
             )
             for i, acc in enumerate(accs):
                 put_sum(dot_index(i, k + 1), acc)
@@ -514,23 +541,22 @@
         for j in range(6):
             for i in range(j + 1):
                 gram[i][j] = gram[j][i] = splat(row, dot_index(i, j))
-        weights = [wide(x) for x in small_solve(gram, mid, rho)]
-
-        def update(s, carry, step=step, weights=weights):
-            r = pl.multiple_of(8 + 8 * s, 8)
+        weights = small_solve(gram, mid, rho)
+
+        def update(r, n, carry, step=step, weights=weights):
             tiles = pl.ds(0, 3 if step == 0 else 2)
             for c in range(2):
-                total = fields[c, tiles, rows8(r), :]
+                total = fields[c, tiles, pl.ds(r, n), :]
                 for k in range(KRYLOV):
-                    total = total + weights[k] * krylov[k, c, tiles, rows8(r), :]
-                fields[c, tiles, rows8(r), :] = total
+                    total = total + weights[k] * krylov[k, c, tiles, pl.ds(r, n), :]
+                fields[c, tiles, pl.ds(r, n), :] = total
             return carry
 
         if step == 0:
             for copy in halo_copies:
                 copy.wait_send()
         lo, hi = strips(2 if step == 0 else 0)
-        lax.fori_loop(lo, hi, update, 0)
+        sweep(lo, hi, update, 0, UPD)
         if step == 0:
             mid, square = basis_of(row, N_DOTS)
 

time: 136 us -> 82.6 us (0.61)
  Pallas kernels: 133 us -> 79.1 us
    pallas_call x1, Pallas kernels: 133 us -> 79.1 us  [on_device(): pl.pallas_call(kernel, out_shape=(jax.ShapeDtypeStruct((2, 256, 256), F32...]
where the time goes in v2:
time: 82.6 us; the launch traced here: 82.4 us
  Pallas kernels  79.1 us (96%)
  local copies, waits for them, and re-layouts  2.62 us (3%)
    pallas_call x1, Pallas kernels, on_device(): pl.pallas_call(kernel, out_shape=(jax.ShapeDtypeStruct((2, 256, 256), F32...  79.1 us
    unnamed x4, local copies, waits for them, and re-layouts  2.62 us

profile of v2, /device:TPU:1, one launch (start us, length us, event | category | flops | bytes accessed | tf_op | source)
XLA Modules:
  0.0 82.4 jit_solution(14456383198938879371)
XLA Ops:
  0.6 79.1 %shard_map.86 = (f32[2,256,256]{2,1,0:T(8,128)}, f32[2,1,2,128,128]{4,3,2,1,0:T(8,128)}) custom-call(s32[2,2]{1,0:T(2,128)} %ice_ref.1, s32[2,2]{1,0:T(2,128)} %owner_ref.1, s32[2,2]{1,0:T(2,128)} %slot_ref.1, f32[2,256,256]{2,1,0:T(8,128)} %vel_ref.1, f32[2,256,256]{2,1,0:T(8,128)} %wind_ref.1, f32[256,256]{1,0:T(8,128)} %strength_ref.1, f32[256,256]{1,0:T(8,128)} %mass_ref.1), custom_call_target="tpu_custom_call" | custom-call | tf_op jit(solution)/shard_map/pallas_call | solution.py:639
  79.8 0.0 copy-start
  79.8 1.9 %copy.11 = f32[2,256,256]{2,1,0:T(8,128)} copy(f32[2,256,256]{2,1,0:T(8,128)} %get-tuple-element.4) | data formatting | bytes 1048576
  81.7 0.0 copy-done
  81.7 0.7 copy.12
Async XLA Ops:
  79.8 1.9 %copy-start = (f32[2,1,2,128,128]{4,3,2,1,0:T(8,128)S(1)}, f32[2,1,2,128,128]{4,3,2,1,0:T(8,128)}, u32[]{:S(2)}) copy-start(f32[2,1,2,128,128]{4,3,2,1,0:T(8,128)} %get-tuple-element.5) | copy-start | bytes 786436

commit v3 on v2

--- a/solution.py
+++ b/solution.py
@@ -25,7 +25,7 @@
 OFFSETS = (0, 22, 44, 66, 86, 106)
 
 VISC = 4
-TAN = 8
+TAN = 19
 VEC = 8
 UPD = 4
 
@@ -180,7 +180,7 @@
     st_vel, st_wind, st_strength, st_mass,
     fields, local, coef, stress, krylov,
     pack_e, pack_w, got_l, got_r, sums,
-    buf_a, buf_b, send_blocks, recv_blocks, held_buf,
+    buf_a, buf_b, send_blocks, recv_blocks, sum_blocks, held_buf,
     in_sem, halo_send, halo_recv, ar_send, ar_recv, held_send, held_recv, out_sem,
 ):
     lat, lon = lax.axis_index("lat"), lax.axis_index("lon")
@@ -188,22 +188,16 @@
     east, west = lax.rem(lon + 1, LON), lax.rem(lon + LON - 1, LON)
     core = lax.rem(lon, 2)
     chip = lon // 2
-    rank_a = lat * 2 + core
-    rank_b = chip
-
-    peers_a = []
-    for i in (4, 5, 2, 3, 6, 7, 1):
-        other = lax.rem(rank_a + i, 8)
-        peers_a.append((other // 2, chip * 2 + lax.rem(other, 2)))
+    rank_b = lat * 16 + chip
+    y, z = chip // 4, lax.rem(chip, 4)
+
+    partner = (lat, chip * 2 + (1 - core))
     peers_b = []
-    for i in (10, 9, 11, 6, 8, 2, 14, 7, 5, 13, 1, 3, 15, 4, 12):
-        peers_b.append((lat, lax.rem(rank_b + i, 16) * 2 + core))
+    shifts = [(i, j, k) for i in range(4) for j in range(4) for k in range(4) if i or j or k]
+    for i, j, k in sorted(shifts, key=lambda d: -sum(min(n, 4 - n) + (n > 0) for n in d)):
+        other = lax.rem(y + j, 4) * 4 + lax.rem(z + k, 4)
+        peers_b.append((lax.rem(lat + i, 4), other * 2 + core))
     halo_peers = [(lat, east), (lat, west), (north, east), (north, west), (south, east), (south, west)]
-
-    barrier = pltpu.get_barrier_semaphore()
-    greeted = peers_b + peers_a + halo_peers
-    for peer in greeted:
-        pl.semaphore_signal(barrier, inc=1, device_id=peer, device_id_type=MESH)
 
     loads = []
     for t in range(2):
@@ -214,85 +208,63 @@
         loads.append(pltpu.make_async_copy(mass_ref.at[:, cols], st_mass.at[t], in_sem.at[6 + t]))
     for copy in loads:
         copy.start()
+
+    barrier = pltpu.get_barrier_semaphore()
+    greeted = peers_b + halo_peers
+    for peer in greeted:
+        pl.semaphore_signal(barrier, inc=1, device_id=peer, device_id_type=MESH)
+
     for copy in loads:
         copy.wait()
 
-    lane8 = lanes((8, 128))
     ice = [[ice_ref[i, j].astype(F32) for j in range(2)] for i in range(2)]
     for half in range(2):
 
         def prepare(s, carry, half=half):
-            src = pl.multiple_of(8 * s, 8)
-            dst = pl.multiple_of(TOP + 8 * s, 8)
+            src = pl.ds(pl.multiple_of(32 * s, 32), 32)
+            dst = pl.ds(pl.multiple_of(TOP + 32 * s, 32), 32)
+            lane = lanes((32, 128))
             for t in range(2):
                 w = ice[half][t]
-                mass = st_mass[t, rows8(src), :] * w
-                v_e = st_vel[0, t, rows8(src), :]
-                v_n = st_vel[1, t, rows8(src), :]
+                mass = st_mass[t, src, :] * w
+                v_e = st_vel[0, t, src, :]
+                v_n = st_vel[1, t, src, :]
                 values = (
                     v_e * w,
                     v_n * w,
-                    st_strength[t, rows8(src), :] * w,
+                    st_strength[t, src, :] * w,
                     mass,
-                    mass * v_e + w * st_wind[0, t, rows8(src), :],
-                    mass * v_n + w * st_wind[1, t, rows8(src), :],
+                    mass * v_e + w * st_wind[0, t, src, :],
+                    mass * v_n + w * st_wind[1, t, src, :],
                 )
                 for f in range(6):
-                    fields[f, t, rows8(dst), :] = values[f]
-                local[0, t, rows8(dst), :] = mass + 0.5 * w
-                local[1, t, rows8(dst), :] = 0.3 * mass
-                local[2, t, rows8(dst), :] = jnp.zeros((8, 128), F32) + 0.5 * w
+                    fields[f, t, dst, :] = values[f]
+                local[0, t, dst, :] = mass + 0.5 * w
+                local[1, t, dst, :] = 0.3 * mass
+                local[2, t, dst, :] = jnp.zeros((32, 128), F32) + 0.5 * w
                 packed = None
                 for f in range(6):
                     turn = (OFFSETS[f] if t == 0 else OFFSETS[f] + WIDTHS[f]) % 128
                     rolled = values[f] if turn == 0 else pltpu.roll(values[f], turn, 1)
-                    packed = rolled if f == 0 else jnp.where(lane8 >= OFFSETS[f], rolled, packed)
-                (pack_w if t == 0 else pack_e)[rows8(src), :] = packed
+                    packed = rolled if f == 0 else jnp.where(lane >= OFFSETS[f], rolled, packed)
+                (pack_w if t == 0 else pack_e)[src, :] = packed
             return carry
 
-        lax.fori_loop(16 * half, 16 * half + 16, prepare, 0)
-
-    pl.semaphore_wait(barrier, len(greeted))
-
-    own_top, own_bot = pl.ds(TOP, HALO), pl.ds(BOT - HALO, HALO)
-    halo_top, halo_bot = pl.ds(TOP - HALO, HALO), pl.ds(BOT, HALO)
-    own_rows = pl.ds(TOP, 256)
-    src_top, src_bot = pl.ds(0, HALO), pl.ds(256 - HALO, HALO)
-    plan = [
-        (fields.at[:, pl.ds(0, 2), own_top, :], fields.at[:, pl.ds(0, 2), halo_bot, :], (north, lon)),
-        (fields.at[:, pl.ds(0, 2), own_bot, :], fields.at[:, pl.ds(0, 2), halo_top, :], (south, lon)),
-        (pack_e.at[src_top, :], got_l.at[halo_bot, :], (north, east)),
-        (pack_w.at[src_top, :], got_r.at[halo_bot, :], (north, west)),
-        (pack_e.at[src_bot, :], got_l.at[halo_top, :], (south, east)),
-        (pack_w.at[src_bot, :], got_r.at[halo_top, :], (south, west)),
-        (pack_e, got_l.at[own_rows, :], (lat, east)),
-        (pack_w, got_r.at[own_rows, :], (lat, west)),
-    ]
-    halo_copies = []
-    for i, (src, dst, peer) in enumerate(plan):
-        copy = pltpu.make_async_remote_copy(
-            src_ref=src, dst_ref=dst, send_sem=halo_send.at[i], recv_sem=halo_recv.at[i],
-            device_id=peer, device_id_type=MESH,
-        )
-        copy.start()
-        halo_copies.append(copy)
-
+        lax.fori_loop(4 * half, 4 * half + 4, prepare, 0)
+
+    first, second, both = pl.ds(0, 3), pl.ds(3, 3), pl.ds(0, 2)
     def reduce_a_start(inst, row):
-        buf_a[inst, rank_a] = row
-        for peer in peers_a:
-            pltpu.make_async_remote_copy(
-                src_ref=buf_a.at[inst, rank_a], dst_ref=buf_a.at[inst, rank_a],
-                send_sem=ar_send.at[inst, 0], recv_sem=ar_recv.at[inst, 0],
-                device_id=peer, device_id_type=MESH,
-            ).start()
+        buf_a[inst, core] = row
+        pltpu.make_async_remote_copy(
+            src_ref=buf_a.at[inst, core], dst_ref=buf_a.at[inst, core],
+            send_sem=ar_send.at[inst, 0], recv_sem=ar_recv.at[inst, 0],
+            device_id=partner, device_id_type=MESH,
+        ).start()
 
     def reduce_b_start(inst):
-        waited = buf_a.at[inst, pl.ds(0, 7)]
+        waited = buf_a.at[inst, 0]
         pltpu.make_async_copy(waited, waited, ar_recv.at[inst, 0]).wait()
-        row = buf_a[inst, 0]
-        for i in range(1, 8):
-            row = row + buf_a[inst, i]
-        buf_b[inst, rank_b] = row
+        buf_b[inst, rank_b] = buf_a[inst, 0] + buf_a[inst, 1]
         for peer in peers_b:
             pltpu.make_async_remote_copy(
                 src_ref=buf_b.at[inst, rank_b], dst_ref=buf_b.at[inst, rank_b],
@@ -301,12 +273,12 @@
             ).start()
 
     def reduce_end(inst):
-        waited = buf_b.at[inst, pl.ds(0, 15)]
+        waited = buf_b.at[inst, pl.ds(0, 63)]
         pltpu.make_async_copy(waited, waited, ar_recv.at[inst, 1]).wait()
-        parts = [buf_b[inst, i] for i in range(16)]
+        parts = [buf_b[inst, pl.ds(8 * i, 8)] for i in range(8)]
         while len(parts) > 1:
             parts = [x + y for x, y in zip(parts[::2], parts[1::2])]
-        return parts[0]
+        return jnp.sum(parts[0], axis=0)
 
     def put_sum(index, acc):
         sums[index : index + 1, :] = jnp.sum(acc, axis=0, keepdims=True)
@@ -319,15 +291,12 @@
         return jnp.sum(spread, axis=0, keepdims=True)
 
     def estimate_pass(alpha):
-        both = pl.ds(0, 2)
-
         def at(c, r):
             flow = fields[c, both, rows8(r), :]
             return flow if alpha is None else flow + alpha * krylov[0, c, both, rows8(r), :]
 
-        def body(i, carry):
+        def one(r, carry):
             diag_acc, spread_acc, ice_acc = carry
-            r = pl.multiple_of(TOP + 8 + 16 * i, 8)
             x_e, x_n = diff_x_rough(at(0, r)), diff_x_rough(at(1, r))
             y_e, y_n = at(0, r + 1) - at(0, r - 1), at(1, r + 1) - at(1, r - 1)
             m2, _, gs, gf, ge = coefficients(x_e + y_n, x_e - y_n, y_e + x_n, fields[2, both, rows8(r), :])
@@ -341,8 +310,13 @@
                 ice_acc + 2.0 * (weight[0] + weight[1]),
             )
 
+        def body(i, carry):
+            for j in range(5):
+                carry = one(pl.multiple_of(TOP + 8 + 80 * i + 16 * j, 8), carry)
+            return carry
+
         zero = jnp.zeros((8, 128), F32)
-        return lax.fori_loop(0, 15, body, (zero, zero, zero))
+        return lax.fori_loop(0, 3, body, (zero, zero, zero))
 
     def basis_of(row, at):
         diag, spread, count = splat(row, at), splat(row, at + 1), splat(row, at + 2)
@@ -352,47 +326,85 @@
 
     for i, acc in enumerate(estimate_pass(None)):
         put_sum(i, acc)
-    reduce_a_start(0, packed_sums(8))
-
-    for copy in halo_copies:
-        copy.wait_recv()
+    first_sums = packed_sums(8)
+
+    pl.semaphore_wait(barrier, len(greeted))
+
+    own_top, own_bot = pl.ds(TOP, HALO), pl.ds(BOT - HALO, HALO)
+    halo_top, halo_bot = pl.ds(TOP - HALO, HALO), pl.ds(BOT, HALO)
+    own_rows = pl.ds(TOP, 256)
+    src_top, src_bot = pl.ds(0, HALO), pl.ds(256 - HALO, HALO)
+    plan = [
+        (fields.at[first, both, own_top, :], fields.at[first, both, halo_bot, :], (north, lon)),
+        (fields.at[first, both, own_bot, :], fields.at[first, both, halo_top, :], (south, lon)),
+        (pack_e.at[src_top, :], got_l.at[halo_bot, :], (north, east)),
+        (pack_w.at[src_top, :], got_r.at[halo_bot, :], (north, west)),
+        (pack_e.at[src_bot, :], got_l.at[halo_top, :], (south, east)),
+        (pack_w.at[src_bot, :], got_r.at[halo_top, :], (south, west)),
+        (pack_e, got_l.at[own_rows, :], (lat, east)),
+        (pack_w, got_r.at[own_rows, :], (lat, west)),
+        (fields.at[second, both, own_top, :], fields.at[second, both, halo_bot, :], (north, lon)),
+        (fields.at[second, both, own_bot, :], fields.at[second, both, halo_top, :], (south, lon)),
+    ]
+    halo_copies = []
+    for i, (src, dst, peer) in enumerate(plan):
+        copy = pltpu.make_async_remote_copy(
+            src_ref=src, dst_ref=dst, send_sem=halo_send.at[i], recv_sem=halo_recv.at[i],
+            device_id=peer, device_id_type=MESH,
+        )
+        copy.start()
+        halo_copies.append(copy)
+
+    reduce_a_start(0, first_sums)
 
     keep_top = jnp.where(lat == 0, 0.0, 1.0).astype(F32)
     keep_bot = jnp.where(lat == LAT - 1, 0.0, 1.0).astype(F32)
 
-    def put_local(t, r, mass):
+    def put_local(t, here, mass):
         w = jnp.where(mass > 0.0, 1.0, 0.0)
-        local[0, t, rows8(r), :] = mass + 0.5 * w
-        local[1, t, rows8(r), :] = 0.3 * mass
-        local[2, t, rows8(r), :] = 0.5 * w
-
-    def unpack(lo, hi, keep):
-        def body(s, carry):
-            r = pl.multiple_of(8 + 8 * s, 8)
-            left, right = got_l[rows8(r), :], got_r[rows8(r), :]
+        local[0, t, here, :] = mass + 0.5 * w
+        local[1, t, here, :] = 0.3 * mass
+        local[2, t, here, :] = 0.5 * w
+
+    def unpack(keep):
+        def body(r, n, carry):
+            here = pl.ds(r, n)
+            left, right = got_l[here, :], got_r[here, :]
+            lane = lanes((n, 128))
             for f in range(6):
                 turn_l = (128 - OFFSETS[f] - WIDTHS[f]) % 128
                 turn_r = (128 - OFFSETS[f]) % 128
                 from_l = left if turn_l == 0 else pltpu.roll(left, turn_l, 1)
                 from_r = right if turn_r == 0 else pltpu.roll(right, turn_r, 1)
-                merged = jnp.where(lane8 < 64, from_r, from_l)
+                merged = jnp.where(lane < 64, from_r, from_l)
                 if keep is not None:
                     merged = merged * keep
-                    for t in range(2):
-                        kept = fields[f, t, rows8(r), :] * keep
-                        fields[f, t, rows8(r), :] = kept
-                        if f == 3:
-                            put_local(t, r, kept)
-                fields[f, 2, rows8(r), :] = merged
+                fields[f, 2, here, :] = merged
                 if f == 3:
-                    put_local(2, r, merged)
+                    put_local(2, here, merged)
             return carry
 
-        lax.fori_loop(lo, hi, body, 0)
-
-    unpack(0, 3, keep_top)
-    unpack(3, 35, None)
-    unpack(35, 38, keep_bot)
+        return body
+
+    def clear_first(top, keep):
+        fields[first, both, pl.ds(top, HALO), :] = fields[first, both, pl.ds(top, HALO), :] * keep
+
+    def clear_second(top, keep):
+        here = pl.ds(top, HALO)
+        for t in range(2):
+            for f in range(3, 6):
+                kept = fields[f, t, here, :] * keep
+                fields[f, t, here, :] = kept
+                if f == 3:
+                    put_local(t, here, kept)
+
+    for copy in halo_copies[:8]:
+        copy.wait_recv()
+    sweep(0, 3, unpack(keep_top), 0, 3)
+    sweep(3, 35, unpack(None), 0, 4)
+    sweep(35, 38, unpack(keep_bot), 0, 3)
+    clear_first(TOP - HALO, keep_top)
+    clear_first(BOT, keep_bot)
 
     reduce_b_start(0)
 
@@ -509,6 +521,11 @@
     mid = square = None
     for step in range(2):
         viscous_pass(3 - step)
+        if step == 0:
+            for copy in halo_copies[8:]:
+                copy.wait_recv()
+            clear_second(TOP - HALO, keep_top)
+            clear_second(BOT, keep_bot)
         accs = vector_pass(residual_at, 0, 3 - step)
         put_sum(0, accs[0])
         if step == 0:
@@ -578,54 +595,73 @@
                 picks[-1].append(jnp.where(hit, 1.0, 0.0).astype(F32))
 
     def choose(s, carry):
-        src = pl.multiple_of(8 * s, 8)
+        src = pl.ds(pl.multiple_of(16 * s, 16), 16)
         for c in range(2):
             blocks = []
             for i in range(2):
                 for j in range(2):
-                    blocks.append(fields[c, j, rows8(pl.multiple_of(TOP + 128 * i + 8 * s, 8)), :])
+                    blocks.append(fields[c, j, pl.ds(pl.multiple_of(TOP + 128 * i + 16 * s, 16), 16), :])
             for slot in range(8):
                 total = blocks[0] * picks[slot][0]
                 for b in range(1, 4):
                     total = total + blocks[b] * picks[slot][b]
-                send_blocks[slot // 2, slot % 2, c, rows8(src), :] = total
+                send_blocks[slot // 2, slot % 2, c, src, :] = total
         return carry
 
-    lax.fori_loop(0, 16, choose, 0)
-
-    held_copies = []
-    for i in (2, 1, 3):
-        other = lax.rem(lat + i, LAT)
+    lax.fori_loop(0, 8, choose, 0)
+
+    opposite = lax.rem(lat + 2, LAT)
+
+    def held_copy(i, src, peer):
         copy = pltpu.make_async_remote_copy(
-            src_ref=send_blocks.at[other], dst_ref=recv_blocks.at[i - 1],
-            send_sem=held_send.at[i - 1], recv_sem=held_recv.at[i - 1],
-            device_id=(other, lon), device_id_type=MESH,
+            src_ref=src, dst_ref=recv_blocks.at[i], send_sem=held_send.at[i], recv_sem=held_recv.at[i],
+            device_id=(peer, lon), device_id_type=MESH,
         )
         copy.start()
-        held_copies.append(copy)
-    for copy in held_copies:
+        return copy
+
+    held_copies = [
+        held_copy(0, send_blocks.at[opposite, 0], south),
+        held_copy(1, send_blocks.at[opposite, 1], north),
+        held_copy(2, send_blocks.at[south, 1], south),
+        held_copy(3, send_blocks.at[north, 0], north),
+    ]
+
+    def merge(i, owner, slot):
+        def body(s, carry):
+            r = pl.ds(pl.multiple_of(32 * s, 32), 32)
+            for c in range(2):
+                sum_blocks[i, c, r, :] = recv_blocks[i, c, r, :] + send_blocks[owner, slot, c, r, :]
+            return carry
+
+        lax.fori_loop(0, 4, body, 0)
+
+    held_copies[0].wait_recv()
+    merge(0, south, 0)
+    held_copies.append(held_copy(4, sum_blocks.at[0], south))
+    held_copies[1].wait_recv()
+    merge(1, north, 1)
+    held_copies.append(held_copy(5, sum_blocks.at[1], north))
+    for copy in held_copies[2:]:
         copy.wait_recv()
 
     def collect(s, carry):
-        r = pl.multiple_of(8 * s, 8)
-        for slot in range(2):
-            for c in range(2):
-                total = send_blocks[lat, slot, c, rows8(r), :]
-                for i in range(3):
-                    total = total + recv_blocks[i, slot, c, rows8(r), :]
-                held_buf[slot, c, rows8(r), :] = total
+        r = pl.ds(pl.multiple_of(32 * s, 32), 32)
+        for c in range(2):
+            held_buf[0, c, r, :] = send_blocks[lat, 0, c, r, :] + (recv_blocks[3, c, r, :] + recv_blocks[4, c, r, :])
+            held_buf[1, c, r, :] = send_blocks[lat, 1, c, r, :] + (recv_blocks[2, c, r, :] + recv_blocks[5, c, r, :])
         return carry
 
-    lax.fori_loop(0, 16, collect, 0)
+    lax.fori_loop(0, 4, collect, 0)
     last = pltpu.make_async_copy(held_buf, held_ref.at[:, 0], out_sem.at[2])
     last.start()
 
     for copy in held_copies:
         copy.wait_send()
     for inst in range(3):
-        sent = buf_a.at[inst, pl.ds(0, 7)]
+        sent = buf_a.at[inst, 0]
         pltpu.make_async_copy(sent, sent, ar_send.at[inst, 0]).wait()
-        sent = buf_b.at[inst, pl.ds(0, 15)]
+        sent = buf_b.at[inst, pl.ds(0, 63)]
         pltpu.make_async_copy(sent, sent, ar_send.at[inst, 1]).wait()
     for copy in outs:
         copy.wait()
@@ -659,18 +695,19 @@
             pltpu.VMEM((ROWS, 128), F32),
             pltpu.VMEM((ROWS, 128), F32),
             pltpu.VMEM((N_SUMS, 128), F32),
-            pltpu.VMEM((3, 8, 1, 128), F32),
-            pltpu.VMEM((3, 16, 1, 128), F32),
+            pltpu.VMEM((3, 2, 1, 128), F32),
+            pltpu.VMEM((3, 64, 1, 128), F32),
             pltpu.VMEM((4, 2, 2, 128, 128), F32),
-            pltpu.VMEM((3, 2, 2, 128, 128), F32),
+            pltpu.VMEM((6, 2, 128, 128), F32),
+            pltpu.VMEM((2, 2, 128, 128), F32),
             pltpu.VMEM((2, 2, 128, 128), F32),
             pltpu.SemaphoreType.DMA((8,)),
-            pltpu.SemaphoreType.DMA((8,)),
-            pltpu.SemaphoreType.DMA((8,)),
+            pltpu.SemaphoreType.DMA((10,)),
+            pltpu.SemaphoreType.DMA((10,)),
             pltpu.SemaphoreType.DMA((3, 2)),
             pltpu.SemaphoreType.DMA((3, 2)),
-            pltpu.SemaphoreType.DMA((3,)),
-            pltpu.SemaphoreType.DMA((3,)),
+            pltpu.SemaphoreType.DMA((6,)),
+            pltpu.SemaphoreType.DMA((6,)),
             pltpu.SemaphoreType.DMA((3,)),
         ],
         compiler_params=pltpu.CompilerParams(

time: 82.6 us -> 73.1 us (0.88)
  Pallas kernels: 79.1 us -> 69.6 us
    pallas_call x1, Pallas kernels: 79.1 us -> 69.6 us  [on_device(): pl.pallas_call(kernel, out_shape=(jax.ShapeDtypeStruct((2, 256, 256), F32...]
where the time goes in v3:
time: 73.1 us; the launch traced here: 72.9 us
  Pallas kernels  69.6 us (95%)
  local copies, waits for them, and re-layouts  2.62 us (4%)
    pallas_call x1, Pallas kernels, on_device(): pl.pallas_call(kernel, out_shape=(jax.ShapeDtypeStruct((2, 256, 256), F32...  69.6 us
    unnamed x4, local copies, waits for them, and re-layouts  2.62 us

profile of v3, /device:TPU:1, one launch (start us, length us, event | category | flops | bytes accessed | tf_op | source)
XLA Modules:
  0.0 72.9 jit_solution(11117356533921008124)
XLA Ops:
  0.6 69.6 %shard_map.86 = (f32[2,256,256]{2,1,0:T(8,128)}, f32[2,1,2,128,128]{4,3,2,1,0:T(8,128)}) custom-call(s32[2,2]{1,0:T(2,128)} %ice_ref.1, s32[2,2]{1,0:T(2,128)} %owner_ref.1, s32[2,2]{1,0:T(2,128)} %slot_ref.1, f32[2,256,256]{2,1,0:T(8,128)} %vel_ref.1, f32[2,256,256]{2,1,0:T(8,128)} %wind_ref.1, f32[256,256]{1,0:T(8,128)} %strength_ref.1, f32[256,256]{1,0:T(8,128)} %mass_ref.1), custom_call_target="tpu_custom_call" | custom-call | tf_op jit(solution)/shard_map/pallas_call | solution.py:675
  70.3 0.0 copy-start
  70.3 1.9 %copy.11 = f32[2,256,256]{2,1,0:T(8,128)} copy(f32[2,256,256]{2,1,0:T(8,128)} %get-tuple-element.4) | data formatting | bytes 1048576
  72.2 0.0 copy-done
  72.2 0.7 copy.12
Async XLA Ops:
  70.3 1.9 %copy-start = (f32[2,1,2,128,128]{4,3,2,1,0:T(8,128)S(1)}, f32[2,1,2,128,128]{4,3,2,1,0:T(8,128)}, u32[]{:S(2)}) copy-start(f32[2,1,2,128,128]{4,3,2,1,0:T(8,128)} %get-tuple-element.5) | copy-start | bytes 786436

commit v4 on v3

--- a/solution.py
+++ b/solution.py
@@ -24,9 +24,9 @@
 WIDTHS = (22, 22, 22, 20, 20, 20)
 OFFSETS = (0, 22, 44, 66, 86, 106)
 
-VISC = 4
+VISC = 10
 TAN = 19
-VEC = 8
+VEC = 32
 UPD = 4
 
 N_DOTS = 21
@@ -180,8 +180,8 @@
     st_vel, st_wind, st_strength, st_mass,
     fields, local, coef, stress, krylov,
     pack_e, pack_w, got_l, got_r, sums,
-    buf_a, buf_b, send_blocks, recv_blocks, sum_blocks, held_buf,
-    in_sem, halo_send, halo_recv, ar_send, ar_recv, held_send, held_recv, out_sem,
+    buf_a, buf_b, send_blocks, recv_blocks, sum_blocks,
+    in_sem, halo_send, halo_recv, ar_send, ar_recv, held_send, held_recv,
 ):
     lat, lon = lax.axis_index("lat"), lax.axis_index("lon")
     north, south = lax.rem(lat + LAT - 1, LAT), lax.rem(lat + 1, LAT)
@@ -290,7 +290,7 @@
         spread = jnp.where(lanes((count, 128)) == sub, total, 0.0)
         return jnp.sum(spread, axis=0, keepdims=True)
 
-    def estimate_pass(alpha):
+    def estimate_pass(alpha, count):
         def at(c, r):
             flow = fields[c, both, rows8(r), :]
             return flow if alpha is None else flow + alpha * krylov[0, c, both, rows8(r), :]
@@ -312,11 +312,11 @@
 
         def body(i, carry):
             for j in range(5):
-                carry = one(pl.multiple_of(TOP + 8 + 80 * i + 16 * j, 8), carry)
+                carry = one(pl.multiple_of(TOP + 8 + 48 * j + 16 * i, 8), carry)
             return carry
 
         zero = jnp.zeros((8, 128), F32)
-        return lax.fori_loop(0, 3, body, (zero, zero, zero))
+        return lax.fori_loop(0, count, body, (zero, zero, zero))
 
     def basis_of(row, at):
         diag, spread, count = splat(row, at), splat(row, at + 1), splat(row, at + 2)
@@ -324,7 +324,7 @@
         mid = diag * inv
         return mid, jnp.maximum(spread * inv - mid * mid, 0.01)
 
-    for i, acc in enumerate(estimate_pass(None)):
+    for i, acc in enumerate(estimate_pass(None, 3)):
         put_sum(i, acc)
     first_sums = packed_sums(8)
 
@@ -548,7 +548,7 @@
                 m1 = mid[:, 0:1]
                 alpha = (g01 + m1 * g00) / (g11 + 2.0 * m1 * g01 + m1 * m1 * g00 + 1e-12)
                 alpha = jnp.broadcast_to(alpha, (8, 128))
-                for i, acc in enumerate(estimate_pass(alpha)):
+                for i, acc in enumerate(estimate_pass(alpha, 1)):
                     put_sum(N_DOTS + i, acc)
 
         reduce_a_start(1 + step, packed_sums(N_SUMS))
@@ -566,7 +566,11 @@
                 total = fields[c, tiles, pl.ds(r, n), :]
                 for k in range(KRYLOV):
                     total = total + weights[k] * krylov[k, c, tiles, pl.ds(r, n), :]
-                fields[c, tiles, pl.ds(r, n), :] = total
+                if step == 0:
+                    fields[c, tiles, pl.ds(r, n), :] = total
+                else:
+                    for t in range(2):
+                        out_ref[c, pl.ds(r - TOP, n), pl.ds(128 * t, 128)] = total[t]
             return carry
 
         if step == 0:
@@ -577,15 +581,6 @@
         if step == 0:
             mid, square = basis_of(row, N_DOTS)
 
-    outs = []
-    for t in range(2):
-        outs.append(
-            pltpu.make_async_copy(
-                fields.at[pl.ds(0, 2), t, own_rows, :], out_ref.at[:, :, pl.ds(128 * t, 128)], out_sem.at[t]
-            )
-        )
-        outs[-1].start()
-
     picks = []
     for s in range(8):
         picks.append([])
@@ -600,7 +595,7 @@
             blocks = []
             for i in range(2):
                 for j in range(2):
-                    blocks.append(fields[c, j, pl.ds(pl.multiple_of(TOP + 128 * i + 16 * s, 16), 16), :])
+                    blocks.append(out_ref[c, pl.ds(pl.multiple_of(128 * i + 16 * s, 16), 16), pl.ds(128 * j, 128)])
             for slot in range(8):
                 total = blocks[0] * picks[slot][0]
                 for b in range(1, 4):
@@ -648,13 +643,11 @@
     def collect(s, carry):
         r = pl.ds(pl.multiple_of(32 * s, 32), 32)
         for c in range(2):
-            held_buf[0, c, r, :] = send_blocks[lat, 0, c, r, :] + (recv_blocks[3, c, r, :] + recv_blocks[4, c, r, :])
-            held_buf[1, c, r, :] = send_blocks[lat, 1, c, r, :] + (recv_blocks[2, c, r, :] + recv_blocks[5, c, r, :])
+            held_ref[0, 0, c, r, :] = send_blocks[lat, 0, c, r, :] + (recv_blocks[3, c, r, :] + recv_blocks[4, c, r, :])
+            held_ref[1, 0, c, r, :] = send_blocks[lat, 1, c, r, :] + (recv_blocks[2, c, r, :] + recv_blocks[5, c, r, :])
         return carry
 
     lax.fori_loop(0, 4, collect, 0)
-    last = pltpu.make_async_copy(held_buf, held_ref.at[:, 0], out_sem.at[2])
-    last.start()
 
     for copy in held_copies:
         copy.wait_send()
@@ -663,23 +656,18 @@
         pltpu.make_async_copy(sent, sent, ar_send.at[inst, 0]).wait()
         sent = buf_b.at[inst, pl.ds(0, 63)]
         pltpu.make_async_copy(sent, sent, ar_send.at[inst, 1]).wait()
-    for copy in outs:
-        copy.wait()
-    last.wait()
 
 
 def on_device(velocity_old, wind_stress, strength, ice_mass, ice_mask, block_owner, block_slot):
     smem = pl.BlockSpec(memory_space=pltpu.SMEM)
     hbm = pl.BlockSpec(memory_space=pl.ANY)
+    vm = pl.BlockSpec(memory_space=pltpu.VMEM)
     field = (3, ROWS, 128)
     velocity, held = pl.pallas_call(
         kernel,
-        out_shape=(
-            jax.ShapeDtypeStruct((2, 256, 256), F32),
-            jax.ShapeDtypeStruct((2, 1, 2, 128, 128), F32),
-        ),
-        in_specs=[smem] * 3 + [hbm] * 4,
-        out_specs=(hbm, hbm),
+        out_shape=(pltpu.VMEM((2, 256, 256), F32), pltpu.VMEM((2, 1, 2, 128, 128), F32)),
+        in_specs=[smem] * 3 + [pl.BlockSpec(memory_space=pltpu.HBM)] * 4,
+        out_specs=(vm, vm),
         scratch_shapes=[
             pltpu.VMEM((2, 2, 256, 128), F32),
             pltpu.VMEM((2, 2, 256, 128), F32),
@@ -700,7 +688,6 @@
             pltpu.VMEM((4, 2, 2, 128, 128), F32),
             pltpu.VMEM((6, 2, 128, 128), F32),
             pltpu.VMEM((2, 2, 128, 128), F32),
-            pltpu.VMEM((2, 2, 128, 128), F32),
             pltpu.SemaphoreType.DMA((8,)),
             pltpu.SemaphoreType.DMA((10,)),
             pltpu.SemaphoreType.DMA((10,)),
@@ -708,13 +695,33 @@
             pltpu.SemaphoreType.DMA((3, 2)),
             pltpu.SemaphoreType.DMA((6,)),
             pltpu.SemaphoreType.DMA((6,)),
-            pltpu.SemaphoreType.DMA((3,)),
         ],
         compiler_params=pltpu.CompilerParams(
             collective_id=0, has_side_effects=True, vmem_limit_bytes=56 * 1024 * 1024
         ),
     )(ice_mask, block_owner, block_slot, velocity_old, wind_stress, strength, ice_mass)
-    return velocity, held
+
+    def pass_on(velocity_ref, held_ref, velocity_out, held_out, sem):
+        copies = [
+            pltpu.make_async_copy(velocity_ref, velocity_out, sem.at[0]),
+            pltpu.make_async_copy(held_ref, held_out, sem.at[1]),
+        ]
+        for copy in copies:
+            copy.start()
+        for copy in copies:
+            copy.wait()
+
+    return pl.pallas_call(
+        pass_on,
+        out_shape=(
+            jax.ShapeDtypeStruct((2, 256, 256), F32),
+            jax.ShapeDtypeStruct((2, 1, 2, 128, 128), F32),
+        ),
+        in_specs=[hbm] * 2,
+        out_specs=(hbm, hbm),
+        scratch_shapes=[pltpu.SemaphoreType.DMA((2,))],
+        compiler_params=pltpu.CompilerParams(vmem_limit_bytes=4 * 1024 * 1024),
+    )(velocity, held)
 
 
 def solution(mesh):

time: 73.1 us -> 68.4 us (0.936)
  local copies, waits for them, and re-layouts: 2.62 us -> 0 us
  Pallas kernels: 69.6 us -> 67.5 us
    unnamed x4 -> x0, local copies, waits for them, and re-layouts: 2.62 us -> none
    pallas_call x1 -> x2, Pallas kernels: 69.6 us -> 67.5 us  [the longest x1 66.6 us: on_device(): pl.pallas_call(kernel, out_shape=(pltpu.VMEM((2, 256, 256), F32), pltpu.V...]
where the time goes in v4:
time: 68.4 us; the launch traced here: 68.3 us
  Pallas kernels  67.5 us (99%)
  between operations  0.8 us (1%)
    pallas_call x1, Pallas kernels, on_device(): pl.pallas_call(kernel, out_shape=(pltpu.VMEM((2, 256, 256), F32), pltpu.V...  66.6 us

profile of v4, /device:TPU:1, one launch (start us, length us, event | category | flops | bytes accessed | tf_op | source)
XLA Modules:
  0.0 68.3 jit_solution(7748692993356333347)
XLA Ops:
  0.6 66.6 %shard_map.86 = (f32[2,256,256]{2,1,0:T(8,128)S(1)}, f32[2,1,2,128,128]{4,3,2,1,0:T(8,128)S(1)}) custom-call(s32[2,2]{1,0:T(2,128)} %ice_ref.1, s32[2,2]{1,0:T(2,128)} %owner_ref.1, s32[2,2]{1,0:T(2,128)} %slot_ref.1, f32[2,256,256]{2,1,0:T(8,128)} %vel_ref.1, f32[2,256,256]{2,1,0:T(8,128)} %wind_ref.1, f32[256,256]{1,0:T(8,128)} %strength_ref.1, ...), custom_call_target="tpu_custom_call" | custom-call | tf_op jit(solution)/shard_map/pallas_call | solution.py:666
  67.2 0.9 %shard_map.87 = (f32[2,256,256]{2,1,0:T(8,128)}, f32[2,1,2,128,128]{4,3,2,1,0:T(8,128)}) custom-call(f32[2,256,256]{2,1,0:T(8,128)S(1)} %get-tuple-element.4.velocity_ref, f32[2,1,2,128,128]{4,3,2,1,0:T(8,128)S(1)} %get-tuple-element.5.held_ref), custom_call_target="tpu_custom_call" | custom-call | tf_op jit(solution)/shard_map/pallas_call | solution.py:714

commit v5 on v4

--- a/solution.py
+++ b/solution.py
@@ -25,9 +25,10 @@
 OFFSETS = (0, 22, 44, 66, 86, 106)
 
 VISC = 10
-TAN = 19
-VEC = 32
+TAN = 10
+VEC = 16
 UPD = 4
+SUB = 2
 
 N_DOTS = 21
 N_SUMS = 24
@@ -41,7 +42,10 @@
     count, rest = divmod(hi - lo, strips)
 
     def step(i, carry):
-        return body(pl.multiple_of(8 + 8 * lo + 8 * strips * i, 8), 8 * strips, carry)
+        first = pl.multiple_of(8 + 8 * lo + 8 * strips * i, 8)
+        for j in range(0, strips, SUB):
+            carry = body(first + 8 * j, 8 * min(SUB, strips - j), carry)
+        return carry
 
     if count:
         carry = lax.fori_loop(0, count, step, carry)
@@ -339,21 +343,22 @@
         (fields.at[first, both, own_bot, :], fields.at[first, both, halo_top, :], (south, lon)),
         (pack_e.at[src_top, :], got_l.at[halo_bot, :], (north, east)),
         (pack_w.at[src_top, :], got_r.at[halo_bot, :], (north, west)),
+        (pack_e, got_l.at[own_rows, :], (lat, east)),
+        (pack_w, got_r.at[own_rows, :], (lat, west)),
         (pack_e.at[src_bot, :], got_l.at[halo_top, :], (south, east)),
         (pack_w.at[src_bot, :], got_r.at[halo_top, :], (south, west)),
-        (pack_e, got_l.at[own_rows, :], (lat, east)),
-        (pack_w, got_r.at[own_rows, :], (lat, west)),
         (fields.at[second, both, own_top, :], fields.at[second, both, halo_bot, :], (north, lon)),
         (fields.at[second, both, own_bot, :], fields.at[second, both, halo_top, :], (south, lon)),
     ]
-    halo_copies = []
-    for i, (src, dst, peer) in enumerate(plan):
+    halo_copies = [None] * 10
+    for i in (2, 3, 6, 7, 0, 1, 4, 5, 8, 9):
+        src, dst, peer = plan[i]
         copy = pltpu.make_async_remote_copy(
             src_ref=src, dst_ref=dst, send_sem=halo_send.at[i], recv_sem=halo_recv.at[i],
             device_id=peer, device_id_type=MESH,
         )
         copy.start()
-        halo_copies.append(copy)
+        halo_copies[i] = copy
 
     reduce_a_start(0, first_sums)
 
@@ -398,20 +403,18 @@
                 if f == 3:
                     put_local(t, here, kept)
 
-    for copy in halo_copies[:8]:
+    for copy in halo_copies[4:6]:
         copy.wait_recv()
-    sweep(0, 3, unpack(keep_top), 0, 3)
     sweep(3, 35, unpack(None), 0, 4)
-    sweep(35, 38, unpack(keep_bot), 0, 3)
+    for copy in halo_copies[:2]:
+        copy.wait_recv()
     clear_first(TOP - HALO, keep_top)
     clear_first(BOT, keep_bot)
 
-    reduce_b_start(0)
-
     def strips(halo):
         return 3 - halo, 35 + halo
 
-    def viscous_pass(halo):
+    def viscous_pass(lo, hi):
         def body(r, n, carry):
             here, up, down = pl.ds(r, n), pl.ds(r + 1, n), pl.ds(r - 1, n)
             x_e, x_n = diff_x(fields[0, :, here, :]), diff_x(fields[1, :, here, :])
@@ -428,7 +431,6 @@
             stress[2, :, here, :] = values[1] * shear
             return carry
 
-        lo, hi = strips(halo)
         sweep(lo, hi, body, 0, VISC)
 
     def tangent_pass(k, halo):
@@ -520,7 +522,17 @@
 
     mid = square = None
     for step in range(2):
-        viscous_pass(3 - step)
+        if step == 0:
+            viscous_pass(4, 34)
+            for copy in halo_copies[2:4] + halo_copies[6:8]:
+                copy.wait_recv()
+            sweep(0, 3, unpack(keep_top), 0, 3)
+            sweep(35, 38, unpack(keep_bot), 0, 3)
+            reduce_b_start(0)
+            viscous_pass(0, 4)
+            viscous_pass(34, 38)
+        else:
+            viscous_pass(*strips(2))
         if step == 0:
             for copy in halo_copies[8:]:
                 copy.wait_recv()

time: 68.4 us -> 67.9 us (level)
  no operation moved by 1% of the time
where the time goes in v5:
time: 67.9 us; the launch traced here: 67.7 us
  Pallas kernels  67.1 us (99%)
    pallas_call x1, Pallas kernels, on_device(): pl.pallas_call(kernel, out_shape=(pltpu.VMEM((2, 256, 256), F32), pltpu.V...  66.2 us

profile of v5, /device:TPU:1, one launch (start us, length us, event | category | flops | bytes accessed | tf_op | source)
XLA Modules:
  0.0 67.7 jit_solution(15374180193726489142)
XLA Ops:
  0.6 66.2 %shard_map.86 = (f32[2,256,256]{2,1,0:T(8,128)S(1)}, f32[2,1,2,128,128]{4,3,2,1,0:T(8,128)S(1)}) custom-call(s32[2,2]{1,0:T(2,128)} %ice_ref.1, s32[2,2]{1,0:T(2,128)} %owner_ref.1, s32[2,2]{1,0:T(2,128)} %slot_ref.1, f32[2,256,256]{2,1,0:T(8,128)} %vel_ref.1, f32[2,256,256]{2,1,0:T(8,128)} %wind_ref.1, f32[256,256]{1,0:T(8,128)} %strength_ref.1, ...), custom_call_target="tpu_custom_call" | custom-call | tf_op jit(solution)/shard_map/pallas_call | solution.py:678
  66.8 0.9 %shard_map.87 = (f32[2,256,256]{2,1,0:T(8,128)}, f32[2,1,2,128,128]{4,3,2,1,0:T(8,128)}) custom-call(f32[2,256,256]{2,1,0:T(8,128)S(1)} %get-tuple-element.4.velocity_ref, f32[2,1,2,128,128]{4,3,2,1,0:T(8,128)S(1)} %get-tuple-element.5.held_ref), custom_call_target="tpu_custom_call" | custom-call | tf_op jit(solution)/shard_map/pallas_call | solution.py:726

commit v6 on v5

--- a/solution.py
+++ b/solution.py
@@ -24,9 +24,9 @@
 WIDTHS = (22, 22, 22, 20, 20, 20)
 OFFSETS = (0, 22, 44, 66, 86, 106)
 
-VISC = 10
-TAN = 10
-VEC = 16
+VISC = 15
+TAN = 19
+VEC = 32
 UPD = 4
 SUB = 2
 

time: 67.9 us -> 64.3 us (0.947)
  Pallas kernels: 67.1 us -> 63.3 us
    pallas_call x1, Pallas kernels: 66.2 us -> 62.4 us  [on_device(): pl.pallas_call(kernel, out_shape=(pltpu.VMEM((2, 256, 256), F32), pltpu.V...]
where the time goes in v6:
time: 64.3 us; the launch traced here: 64.1 us
  Pallas kernels  63.3 us (98%)
  between operations  0.8 us (1%)
    pallas_call x1, Pallas kernels, on_device(): pl.pallas_call(kernel, out_shape=(pltpu.VMEM((2, 256, 256), F32), pltpu.V...  62.4 us

profile of v6, /device:TPU:1, one launch (start us, length us, event | category | flops | bytes accessed | tf_op | source)
XLA Modules:
  0.0 64.1 jit_solution(6094546315798085593)
XLA Ops:
  0.6 62.4 %shard_map.86 = (f32[2,256,256]{2,1,0:T(8,128)S(1)}, f32[2,1,2,128,128]{4,3,2,1,0:T(8,128)S(1)}) custom-call(s32[2,2]{1,0:T(2,128)} %ice_ref.1, s32[2,2]{1,0:T(2,128)} %owner_ref.1, s32[2,2]{1,0:T(2,128)} %slot_ref.1, f32[2,256,256]{2,1,0:T(8,128)} %vel_ref.1, f32[2,256,256]{2,1,0:T(8,128)} %wind_ref.1, f32[256,256]{1,0:T(8,128)} %strength_ref.1, ...), custom_call_target="tpu_custom_call" | custom-call | tf_op jit(solution)/shard_map/pallas_call | solution.py:678
  63.1 0.9 %shard_map.87 = (f32[2,256,256]{2,1,0:T(8,128)}, f32[2,1,2,128,128]{4,3,2,1,0:T(8,128)}) custom-call(f32[2,256,256]{2,1,0:T(8,128)S(1)} %get-tuple-element.4.velocity_ref, f32[2,1,2,128,128]{4,3,2,1,0:T(8,128)S(1)} %get-tuple-element.5.held_ref), custom_call_target="tpu_custom_call" | custom-call | tf_op jit(solution)/shard_map/pallas_call | solution.py:726
